TPU v7x, 512 devices: a whole 4x4x16 slice. The times are simulated.
512 devices in a mesh: row: 64 (over z_lo, x, core), col: 8 (over z_hi, y).
Axes of the slice: x: 4, y: 4, z: 16 (z_hi: 2, z_lo: 8; z = z_hi * 8 + z_lo), core: 2. Of those that a mesh axis runs over, the one named last changes fastest.
Arguments:
- node_features: bfloat16 [65536, 128], P(('row', 'col')), may hold values from -6 to 6
- tile_values: bfloat16 [64, 8, 112, 128, 128], P('row', 'col'), may hold values from -0.046875 to 0.046875
- tile_rows: int32 [64, 8, 112], P('row', 'col'), may hold values from 0 to 7
- tile_cols: int32 [64, 8, 112], P('row', 'col'), may hold values from 0 to 63
- weight_self: bfloat16 [128, 256], replicated, may hold values from -0.5 to 0.5
- weight_neighbour: bfloat16 [128, 256], replicated, may hold values from -0.5 to 0.5
- node_bias: float32 [256], replicated, may hold values from -4 to 4
- output_grad: bfloat16 [65536, 256], P(('row', 'col')), may hold values from -6 to 6
Outputs:
- out_features: bfloat16 [65536, 256], P(('row', 'col'))
- input_grad: bfloat16 [65536, 128], P(('row', 'col'))
- grad_self: float32 [128, 256], replicated
- grad_neighbour: float32 [128, 256], replicated
- grad_bias: float32 [256], replicated
All inputs are finite; a program needn't handle non-finite values.
Results may differ from a plain program's by a relative error of at most 0.015.
Values may be sent and summed in bfloat16 or wider, within the bound.
A program may use at most 64 MiB of HBM per device.

v0:
```python
import jax
import jax.numpy as jnp
from jax import lax
from jax.sharding import PartitionSpec as P


def collect_tiles(tile_block, row_index, col_index, panels, blocks):
    picked = jnp.take(panels, col_index, axis=0)
    product = jnp.einsum("tij,tjf->tif", tile_block, picked, preferred_element_type=jnp.float32)
    placement = (row_index[:, None] == jnp.arange(blocks, dtype=jnp.int32)[None, :]).astype(
        jnp.float32
    )
    return jnp.einsum("tr,tif->rif", placement, product).reshape(blocks * 128, -1)


def spread_tiles(tile_block, row_index, col_index, grad_blocks, blocks):
    picked = jnp.take(grad_blocks, row_index, axis=0)
    product = jnp.einsum("tij,tif->tjf", tile_block, picked, preferred_element_type=jnp.float32)
    placement = (col_index[:, None] == jnp.arange(blocks, dtype=jnp.int32)[None, :]).astype(
        jnp.float32
    )
    return jnp.einsum("tc,tjf->cjf", placement, product).reshape(blocks * 128, -1)


def node_preact(features, neighbour_sum, weight_self, weight_neighbour, node_bias):
    return (
        jnp.dot(features, weight_self, preferred_element_type=jnp.float32)
        + jnp.dot(neighbour_sum, weight_neighbour, preferred_element_type=jnp.float32)
        + node_bias
    )


def preact_grad(preact, output_grad):
    sigmoid_v = jax.nn.sigmoid(preact)
    return (
        output_grad.astype(jnp.float32) * sigmoid_v * (1.0 + preact * (1.0 - sigmoid_v))
    ).astype(jnp.bfloat16)


def times_transpose(left, weight):
    return lax.dot_general(
        left, weight, (((1,), (1,)), ((), ())), preferred_element_type=jnp.float32
    )


def inner_rows(left, right):
    return lax.dot_general(
        left, right, (((0,), (0,)), ((), ())), preferred_element_type=jnp.float32
    )


def body(
    node_features,
    tile_values,
    tile_rows,
    tile_cols,
    weight_self,
    weight_neighbour,
    node_bias,
    output_grad,
):
    rows_dev, feat_width = node_features.shape
    col_count = lax.axis_size("col")
    row_count = lax.axis_size("row")
    row_blocks = col_count * rows_dev // 128
    col_blocks = row_count * rows_dev // 128
    tile_block = tile_values[0, 0]
    row_index = tile_rows[0, 0]
    col_index = tile_cols[0, 0]
    panels = lax.all_gather(node_features, "row", axis=0, tiled=True)
    partial_sum = collect_tiles(
        tile_block, row_index, col_index, panels.reshape(col_blocks, 128, feat_width), row_blocks
    )
    pieces = lax.all_to_all(
        partial_sum.reshape(col_count, rows_dev, feat_width),
        "col",
        split_axis=0,
        concat_axis=0,
        tiled=True,
    )
    neighbour_sum = jnp.sum(pieces, axis=0).astype(jnp.bfloat16)
    preact = node_preact(node_features, neighbour_sum, weight_self, weight_neighbour, node_bias)
    out_features = jax.nn.silu(preact).astype(jnp.bfloat16)
    pre_grad = preact_grad(preact, output_grad)
    sum_grad = times_transpose(pre_grad, weight_neighbour).astype(jnp.bfloat16)
    shard_grad = lax.all_gather(sum_grad, "col", axis=0, tiled=True)
    column_terms = spread_tiles(
        tile_block,
        row_index,
        col_index,
        shard_grad.reshape(row_blocks, 128, feat_width),
        col_blocks,
    )
    neighbour_grad = lax.psum_scatter(column_terms, "row", scatter_dimension=0, tiled=True)
    input_grad = (times_transpose(pre_grad, weight_self) + neighbour_grad).astype(jnp.bfloat16)
    grad_bias, grad_self, grad_neighbour = lax.psum(
        (
            jnp.sum(pre_grad.astype(jnp.float32), axis=0),
            inner_rows(node_features, pre_grad),
            inner_rows(neighbour_sum, pre_grad),
        ),
        ("row", "col"),
    )
    return (out_features, input_grad, grad_self, grad_neighbour, grad_bias)


def solution(mesh):
    placed = (
        P(("row", "col"), None),
        P("row", "col", None, None, None),
        P("row", "col", None),
        P("row", "col", None),
        P(),
        P(),
        P(),
        P(("row", "col"), None),
    )
    return jax.shard_map(
        body,
        mesh=mesh,
        in_specs=placed,
        out_specs=(P(("row", "col"), None), P(("row", "col"), None), P(), P(), P()),
        check_vma=False,
    )
```

profile of v0, /device:TPU:24, one launch (start us, length us, event | category | flops | bytes accessed | tf_op | source)
XLA Modules:
  0.0 1185.1 jit_solution(13457324102045868030)
XLA Ops:
  7.2 0.0 copy-start
  7.2 0.0 all-gather.2.cloned.1.call-start
  7.2 0.7 all-gather.2.cloned.1.call-update
  7.9 0.7 fusion.25
  8.6 0.7 compare_and_fusion.1
  9.2 125.8 %all-gather.2.cloned.1.call-done = bf16[8192,128]{1,0:T(8,128)(2,1)} async-done(((bf16[128,128]{1,0:T(8,128)(2,1)}), bf16[8192,128]{1,0:T(8,128)(2,1)}) %all-gather.2.cloned.1.call-update) | async-done | bytes 2097168 | tf_op jit(solution)/shard_map/all_gather | solution.py:70
  135.1 4.4 gather_fusion
  139.5 7.8 fusion.6
  147.4 0.0 copy-start.3
  147.4 6.3 copy.18
  153.6 0.0 copy-start.1
  153.6 0.0 copy-start.2
  153.6 0.0 copy-start.5
  153.6 0.0 copy-start.6
  153.6 0.0 copy-done.3
  153.6 2.7 fusion.2
  156.3 0.9 copy.15
  157.2 10.8 all-to-all-start
  168.0 0.0 all-reduce.3.cloned.1.call-start
  168.0 0.0 copy-done.1
  168.0 0.0 copy-done.2
  168.0 0.1 fusion.29
  168.2 16.7 %all-to-all-done = f32[8,128,128]{2,1,0:T(8,128)S(1)} async-done(((f32[8,128,128]{2,1,0:T(8,128)}), f32[8,128,128]{2,1,0:T(8,128)S(1)}, u32[]{:S(2)}, u32[]{:S(2)}) %all-to-all-start) | async-done | bytes 524320 | tf_op jit(solution)/shard_map/all_to_all | solution.py:74
  184.9 0.0 copy-done
  184.9 0.0 copy-done.5
  184.9 0.0 copy-done.6
  184.9 0.8 convert_reduce_fusion
  185.8 0.2 convolution_convert_fusion
  186.0 0.8 convolution_bitcast_fusion
  186.8 0.9 fusion.30
  187.7 63.3 %all_gather.7 = bf16[1024,128]{1,0:T(8,128)(2,1)S(1)} all-gather(bf16[128,128]{1,0:T(8,128)(2,1)S(1)} %convolution_convert_fusion), channel_id=1, replica_groups=mesh['row'=64,'col'=8] {'col'}, dimensions={0}, use_global_device_ids=true | all-gather | bytes 294912 | tf_op jit(solution)/shard_map/all_gather | solution.py:86
  250.9 2.9 gather_fusion.1
  253.8 6.5 fusion.4
  260.3 0.0 copy-start.4
  260.3 6.3 copy.19
  266.5 0.0 all-reduce.3.cloned.1.call-update
  266.5 0.0 reduce-scatter.2.cloned.1.call-start
  266.6 0.0 copy-done.4
  266.6 2.7 fusion
  269.3 4.4 copy.16
  273.7 0.0 reduce-scatter.2.cloned.1.call-update
  273.7 115.9 %psum.23 = f32[256]{0:T(256)} all-reduce(f32[256]{0:T(256)S(1)} %get-tuple-element.17), channel_id=1, replica_groups=mesh['row'=64,'col'=8] {'row','col'}, use_global_device_ids=true, to_apply=%region_5.6 | all-reduce | flops 256 | bytes 2048 | tf_op jit(solution)/shard_map/psum | solution.py:96
  389.6 343.6 %all-reduce.3.cloned.1.call-done = (f32[128,256]{0,1:T(8,128)}, f32[128,256]{1,0:T(8,128)}) async-done(((f32[128,256]{0,1:T(8,128)}, f32[128,256]{1,0:T(8,128)}), (f32[128,256]{0,1:T(8,128)}, f32[128,256]{1,0:T(8,128)})) %all-reduce.3.cloned.1.call-update) | async-done | bytes 262160 | tf_op jit(solution)/shard_map/psum | solution.py:96
  733.2 1.7 copy.17
  734.9 440.4 %reduce-scatter.2.cloned.1.call-done = f32[128,128]{1,0:T(8,128)} async-done(((f32[8192,128]{1,0:T(8,128)}), f32[128,128]{1,0:T(8,128)}) %reduce-scatter.2.cloned.1.call-update) | async-done | bytes 65552 | tf_op jit(solution)/shard_map/reduce_scatter | solution.py:94
  1175.3 1.6 fusion.15
  1177.0 1.6 copy.22
  (5 shorter events, 0.1 us)
Async XLA Ops:
  7.2 177.8 %copy-start = (bf16[128,256]{1,0:T(8,128)(2,1)S(1)}, bf16[128,256]{1,0:T(8,128)(2,1)}, u32[]{:S(2)}) copy-start(bf16[128,256]{1,0:T(8,128)(2,1)} %param.13) | copy-start | bytes 196612
  7.2 127.9 %all-gather.2.cloned.1.call-start = ((), (), s32[]{:S(2)}) async-start(), calls=%async_computation.2 | async-start | bytes 2129920 | tf_op jit(solution)/shard_map/all_gather | solution.py:70
  147.4 6.3 copy-start.3
  153.6 14.4 %copy-start.1 = (bf16[128,128]{1,0:T(8,128)(2,1)S(1)}, bf16[128,128]{1,0:T(8,128)(2,1)}, u32[]{:S(2)}) copy-start(bf16[128,128]{1,0:T(8,128)(2,1)} %param.8) | copy-start | bytes 98308
  153.6 14.4 %copy-start.2 = (bf16[128,256]{1,0:T(8,128)(2,1)S(1)}, bf16[128,256]{1,0:T(8,128)(2,1)}, u32[]{:S(2)}) copy-start(bf16[128,256]{1,0:T(8,128)(2,1)} %param.12) | copy-start | bytes 196612
  153.6 31.3 %copy-start.5 = (bf16[128,256]{1,0:T(8,128)(2,1)S(1)}, bf16[128,256]{1,0:T(8,128)(2,1)}, u32[]{:S(2)}) copy-start(bf16[128,256]{1,0:T(8,128)(2,1)} %param.15) | copy-start | bytes 196612
  153.6 31.3 %copy-start.6 = (f32[256]{0:T(256)S(1)}, f32[256]{0:T(256)}, u32[]{:S(2)}) copy-start(f32[256]{0:T(256)} %param.14) | copy-start | bytes 3076
  157.2 27.7 %all-to-all-start = ((f32[8,128,128]{2,1,0:T(8,128)}), f32[8,128,128]{2,1,0:T(8,128)S(1)}, u32[]{:S(2)}, u32[]{:S(2)}) async-start(f32[8,128,128]{2,1,0:T(8,128)} %copy.15), calls=%async_computation | async-start | bytes 1048576 | tf_op jit(solution)/shard_map/all_to_all | solution.py:74
  168.0 565.3 %all-reduce.3.cloned.1.call-start = ((), (), s32[]{:S(2)}) async-start(), calls=%async_computation.4 | async-start | bytes 524288 | tf_op jit(solution)/shard_map/psum | solution.py:96
  260.3 6.3 copy-start.4
  266.5 908.8 %reduce-scatter.2.cloned.1.call-start = ((), (), s32[]{:S(2)}) async-start(), calls=%async_computation.3 | async-start | bytes 4259840 | tf_op jit(solution)/shard_map/reduce_scatter | solution.py:94
Sparse Core Ops, SparseCore 0:
  10.2 124.8 all-gather.1
  266.7 466.5 all-reduce.2
  736.3 438.9 reduce-scatter.1
where the time goes:
time: 1190 us
  waiting for transfers between devices  927 us (78%)
  blocking collectives  179 us (15%)
  local copies, waits for them, and re-layouts  28.4 us (2%)
  matrix products  24.2 us (2%)
  between operations  13.9 us (1%)
    reduce_scatter x1, waiting for transfers between devices, body(): lax.psum_scatter(column_terms, 'row', scatter_dimension=0, tiled=True)  440 us
    psum x1, waiting for transfers between devices, body(): lax.psum((jnp.sum(pre_grad.astype(jnp.float32), axis=0), inner_rows(node_...  344 us
    all_gather x1, waiting for transfers between devices, body(): panels = lax.all_gather(node_features, 'row', axis=0, tiled=True)  126 us
    psum x1, blocking collectives, body(): lax.psum((jnp.sum(pre_grad.astype(jnp.float32), axis=0), inner_rows(node_...  116 us
    all_gather x1, blocking collectives, body(): shard_grad = lax.all_gather(sum_grad, 'col', axis=0, tiled=True)  63.3 us
  transfers between devices with their start and end apart: 4, of which 4 were waited for; matrix products, arithmetic and copies ran while one was open for 1% of the time, Pallas kernels for 0%

commit v1 on v0

v1 whole, which is shorter than its diff:
```python
import functools

import jax
import jax.numpy as jnp
from jax import lax
from jax.experimental import pallas as pl
from jax.experimental.pallas import tpu as pltpu
from jax.sharding import PartitionSpec as P

MESH = pl.DeviceIdType.MESH
BLK = 128
F32 = jnp.float32
BF16 = jnp.bfloat16
VMEM_LIMIT = 64 * 2**20

NX, NC = 4, 2
NY = 4


def dot_nn(a, b):
    return lax.dot_general(a, b, (((1,), (0,)), ((), ())), preferred_element_type=F32)


def dot_nt(a, b):
    return lax.dot_general(a, b, (((1,), (1,)), ((), ())), preferred_element_type=F32)


def dot_tn(a, b):
    return lax.dot_general(a, b, (((0,), (0,)), ((), ())), preferred_element_type=F32)


class Links:
    def __init__(self, send_sems, recv_sems):
        self.send_sems, self.recv_sems, self.copies = send_sems, recv_sems, []

    def send(self, src, dst, device_id):
        at = len(self.copies)
        copy = pltpu.make_async_remote_copy(
            src_ref=src,
            dst_ref=dst,
            send_sem=self.send_sems.at[at],
            recv_sem=self.recv_sems.at[at],
            device_id=device_id,
            device_id_type=MESH,
        )
        copy.start()
        self.copies.append(copy)
        return copy

    def finish(self):
        for copy in self.copies:
            copy.wait_send()


def send_sorted(block, carried, n_blocks, index, at):
    tiles = block.shape[1]
    shape = (tiles, tiles)
    down = lax.broadcasted_iota(jnp.int32, shape, 0)
    across = lax.broadcasted_iota(jnp.int32, shape, 1)

    def turned(line):
        return jnp.sum(jnp.where(down == across, line, 0), axis=1, keepdims=True)

    block_down, carried_down = turned(block), turned(carried)
    before = (block < block_down) | ((block == block_down) & (across < down))
    rank = jnp.sum(before.astype(jnp.int32), axis=1, keepdims=True)
    goes_on = jnp.sum(
        ((block == block_down) & (across < down)).astype(jnp.int32), axis=1, keepdims=True
    )
    hot = rank == across

    def sorted_line(values):
        return jnp.sum(jnp.where(hot, values, 0), axis=0, keepdims=True)

    index[at : at + 1, :tiles] = sorted_line(down)
    index[at + 1 : at + 2, :tiles] = sorted_line(carried_down)
    index[at + 2 : at + 3, :tiles] = sorted_line(jnp.minimum(goes_on, 1))
    ids = lax.broadcasted_iota(jnp.int32, (tiles, n_blocks), 1)
    up_to = jnp.sum((block_down <= ids).astype(jnp.int32), axis=0, keepdims=True)
    held = jnp.sum((block_down == ids).astype(jnp.int32), axis=0, keepdims=True)
    index[at + 3 : at + 4, :n_blocks] = jnp.maximum(up_to - 1, 0)
    index[at + 4 : at + 5, :n_blocks] = jnp.minimum(held, 1)


def kernel(
    nz,
    tiles,
    x_hbm,
    ws_hbm,
    wn_hbm,
    bias_hbm,
    og_hbm,
    rows_hbm,
    cols_hbm,
    tiles_hbm,
    out_hbm,
    ingrad_hbm,
    gself_hbm,
    gneigh_hbm,
    gbias_hbm,
    out_ref,
    ingrad_ref,
    gself_ref,
    gneigh_ref,
    gbias_ref,
    ws_ref,
    wn_ref,
    bias_ref,
    og_ref,
    rows_ref,
    cols_ref,
    index_buf,
    index,
    tile_buf,
    panels,
    runs,
    self_pre,
    self_grad,
    y_send,
    y_recv,
    zh_send,
    zh_recv,
    gt,
    core_send,
    core_recv,
    far_send,
    far_recv,
    near_send,
    near_recv,
    quad_send,
    quad_recv,
    pair_send,
    pair_recv,
    wy_send,
    wy_recv,
    wz_send,
    wz_recv,
    wh_send,
    wh_recv,
    wx_recv,
    wc_send,
    wc_recv,
    w_out,
    load_sems,
    store_sems,
    send_sems,
    recv_sems,
):
    half = nz // 2
    n_cols = nz * NX * NC
    n_rows = 2 * NY
    row = lax.axis_index("row")
    col = lax.axis_index("col")
    core = lax.rem(row, NC)
    x = lax.rem(row // NC, NX)
    z = row // (NC * NX)
    zq = z // half
    zi = lax.rem(z, half)
    y = lax.rem(col, NY)
    zh = col // NY
    other = 1 - core

    def at_row(z_to, x_to, core_to):
        return {"row": (z_to * NX + x_to) * NC + core_to, "col": col}

    def at_col(zh_to, y_to):
        return {"row": row, "col": zh_to * NY + y_to}

    def turn_z(d):
        return lax.rem(z + d, nz)

    def turn_zi(d):
        return lax.rem(zi + d, half)

    def turn_x(d):
        return lax.rem(x + d, NX)

    def turn_y(d):
        return lax.rem(y + d, NY)

    def to_z(d):
        return at_row(turn_z(d), x, core)

    def to_mate(e):
        return at_row(zq * half + turn_zi(e), x, core)

    def to_x(d):
        return at_row(z, turn_x(d), core)

    def to_y(d):
        return at_col(zh, turn_y(d))

    to_pair = at_row((1 - zq) * half + zi, x, core)
    to_core = at_row(z, x, other)
    to_zh = at_col(1 - zh, y)
    mates = [e for e in (1, half - 1) if e] + list(range(2, half - 1))
    mates = list(dict.fromkeys(mates))

    ord_r, pan, keep_r, end_r, has_r, ord_c, grow, keep_c, end_c, has_c = range(10)

    def slot(core_of, x_of, z_of):
        return (core_of * NX + x_of) * nz + z_of

    own = slot(core, x, z)
    loads = []
    for src, dst in (
        (x_hbm, panels.at[own]),
        (rows_hbm, rows_ref),
        (cols_hbm, cols_ref),
        (ws_hbm, ws_ref),
        (bias_hbm, bias_ref),
        (tiles_hbm.at[0, 0], tile_buf),
        (wn_hbm, wn_ref),
        (og_hbm, og_ref),
    ):
        loads.append(pltpu.make_async_copy(src, dst, load_sems.at[len(loads)]))
        loads[-1].start()
    load_x, load_rows, load_cols, load_ws, load_bias, load_tiles, load_wn, load_og = loads

    barrier = pltpu.get_barrier_semaphore()
    partners = [to_z(d) for d in range(1, nz)] + [to_x(d) for d in range(1, NX)]
    partners += [to_y(d) for d in range(1, NY)] + [to_core, to_zh]
    for partner in partners:
        pl.semaphore_signal(barrier, inc=1, device_id=partner, device_id_type=MESH)
    load_x.wait()
    pl.semaphore_wait(barrier, len(partners))

    links = Links(send_sems, recv_sems)
    stores = []

    def store(src, dst):
        stores.append(pltpu.make_async_copy(src, dst, store_sems.at[len(stores)]))
        stores[-1].start()

    def panel_to(slot_at, device_id):
        return links.send(panels.at[slot_at], panels.at[slot_at], device_id)

    pair_copy = panel_to(own, to_pair)
    z_copies = {e: panel_to(own, to_mate(e)) for e in mates}
    pair_z = (1 - zq) * half + zi
    relayed = {}

    def mate_z(e, q):
        return q * half + turn_zi(half - e)

    arrivals = [(z, None)] + [(mate_z(e, zq), z_copies[e]) for e in mates[:2]]
    arrivals += [(pair_z, pair_copy)] + [(mate_z(e, zq), z_copies[e]) for e in mates[2:]]
    arrivals += [(mate_z(e, 1 - zq), e) for e in mates]
    plus, minus, far, crossed = {}, {}, {}, []

    def cross(slot_at):
        crossed.append(panel_to(slot_at, to_core))

    def own_step(i):
        z_of, copy = arrivals[i]
        here = slot(core, x, z_of)
        if copy is not None:
            (relayed[copy] if isinstance(copy, int) else copy).wait_recv()
        if copy is pair_copy:
            for e in mates:
                relayed[e] = panel_to(here, to_mate(e))
        plus[i] = panel_to(here, to_x(1))
        minus[i] = panel_to(here, to_x(NX - 1))
        cross(here)

    def near_step(i):
        z_of = arrivals[i][0]
        from_minus = slot(core, turn_x(NX - 1), z_of)
        from_plus = slot(core, turn_x(1), z_of)
        plus[i].wait_recv()
        if i % 2 == 0:
            far[i] = panel_to(from_minus, to_x(1))
        cross(from_minus)
        minus[i].wait_recv()
        if i % 2 == 1:
            far[i] = panel_to(from_plus, to_x(NX - 1))
        cross(from_plus)

    def far_step(i):
        far[i].wait_recv()
        cross(slot(core, turn_x(2), arrivals[i][0]))

    def prepare():
        load_rows.wait()
        load_cols.wait()
        rows = rows_ref[...]
        cols = cols_ref[...]
        slots = slot(cols & (NC - 1), (cols // NC) & (NX - 1), cols // (NC * NX))
        send_sorted(rows, slots, n_rows, index_buf, 0)
        send_sorted(slots, rows, n_cols, index_buf, 5)
        index_copy = pltpu.make_async_copy(index_buf, index, load_sems.at[len(loads)])
        index_copy.start()
        load_ws.wait()
        load_bias.wait()
        self_pre[...] = dot_nn(panels[own], ws_ref[...]) + bias_ref[...]
        index_copy.wait()

    for i in range(nz + 2):
        if i < nz:
            own_step(i)
        if i == 0:
            prepare()
        if 0 <= i - 1 < nz:
            near_step(i - 1)
        if 0 <= i - 2 < nz:
            far_step(i - 2)
    load_tiles.wait()
    load_wn.wait()
    load_og.wait()
    for copy in crossed:
        copy.wait_recv()

    step = 8

    def collect(k, acc):
        for u in range(step):
            n = k * step + u
            term = dot_nn(tile_buf[index[ord_r, n]], panels[index[pan, n]])
            acc = acc * index[keep_r, n].astype(F32) + term
            runs[n] = acc
        return acc

    lax.fori_loop(0, tiles // step, collect, jnp.zeros((BLK, BLK), F32))

    parts = 2
    width = BLK // parts

    def lines(p):
        return slice(p * width, (p + 1) * width)

    def row_sum(r, p):
        return runs[index[end_r, r], lines(p), :] * index[has_r, r].astype(F32)

    y_copies, zh_copies = {}, {}
    for p in range(parts):
        for d in (2, 1, 3):
            for h in range(2):
                y_send[p, d - 1, h] = row_sum(h * NY + turn_y(d), p).astype(BF16)
            y_copies[p, d] = links.send(y_send.at[p, d - 1], y_recv.at[p, d - 1], to_y(d))
    for p in range(parts):
        theirs = row_sum((1 - zh) * NY + y, p)
        for d in (1, 3, 2):
            y_copies[p, d].wait_recv()
            theirs = theirs + y_recv[p, d - 1, 1 - zh].astype(F32)
        zh_send[p] = theirs.astype(BF16)
        zh_copies[p] = links.send(zh_send.at[p], zh_recv.at[p], to_zh)
    mine = []
    for p in range(parts):
        total_here = row_sum(zh * NY + y, p)
        for d in (1, 3, 2):
            total_here = total_here + y_recv[p, d - 1, zh].astype(F32)
        mine.append(total_here)
    for p in range(parts):
        zh_copies[p].wait_recv()
        mine[p] = (mine[p] + zh_recv[p].astype(F32)).astype(BF16)
    sums = jnp.concatenate(mine, axis=0)

    pre = self_pre[...] + dot_nn(sums, wn_ref[...])
    sig = 1.0 / (1.0 + jnp.exp(-pre))
    pre_grad = (og_ref[...].astype(F32) * sig * (1.0 + pre * (1.0 - sig))).astype(BF16)

    me = zh * NY + y
    they = (1 - zh) * NY + y
    gt[me] = dot_nt(wn_ref[...], pre_grad).astype(BF16)

    def gt_part(r, p):
        return gt.at[r, pl.ds(p * width, width)]

    zh_gt = [links.send(gt_part(me, p), gt_part(me, p), to_zh) for p in range(parts)]
    gt_copies = [links.send(gt.at[me], gt.at[me], to_y(d)) for d in (2, 1, 3)]
    out_ref[...] = (pre * sig).astype(BF16)
    store(out_ref, out_hbm)
    self_grad[...] = dot_nt(ws_ref[...], pre_grad)

    wide_self = dot_tn(panels[own], pre_grad).astype(BF16)
    wide_neigh = dot_tn(sums, pre_grad).astype(BF16)
    for q, block in enumerate(
        (wide_self[:, :BLK], wide_self[:, BLK:], wide_neigh[:, :BLK], wide_neigh[:, BLK:])
    ):
        wy_send[q, :BLK] = block
    bias_sum = jnp.sum(pre_grad.astype(F32), axis=0, keepdims=True)
    spot = lax.broadcasted_iota(jnp.int32, (16, BLK), 0)
    bias_rows = jnp.where(
        spot == 0, bias_sum[:, :BLK], jnp.where(spot == 1, bias_sum[:, BLK:], 0.0)
    ).astype(BF16)
    for q in range(4):
        wy_send[q, BLK:] = bias_rows
    wy_recv[y] = wy_send[y]

    for p in range(parts):
        zh_gt[p].wait_recv()
        gt_copies += [links.send(gt_part(they, p), gt_part(they, p), to_y(d)) for d in (2, 1, 3)]
    wy_copies = [links.send(wy_send.at[turn_y(d)], wy_recv.at[y], to_y(d)) for d in (2, 1, 3)]
    for copy in gt_copies:
        copy.wait_recv()

    def spread(k, acc):
        for u in range(step):
            n = k * step + u
            term = dot_nn(gt[index[grow, n]], tile_buf[index[ord_c, n]])
            acc = acc * index[keep_c, n].astype(F32) + term
            runs[n] = acc
        return acc

    steps = tiles // step
    acc = lax.fori_loop(0, steps // 2, spread, jnp.zeros((BLK, BLK), F32))

    for copy in wy_copies:
        copy.wait_recv()
    w_sum = wy_recv[0].astype(F32)
    for q in range(1, NY):
        w_sum = w_sum + wy_recv[q].astype(F32)
    part = BLK // nz
    for q in range(nz):
        wz_send[q, :part] = w_sum[q * part : (q + 1) * part]
        wz_send[q, part:] = w_sum[BLK : BLK + 8]
    wz_recv[z] = wz_send[z]
    wz_copies = [links.send(wz_send.at[turn_z(d)], wz_recv.at[z], to_z(d)) for d in range(1, nz)]

    lax.fori_loop(steps // 2, steps, spread, acc)

    def chunk(core_of, d):
        return slot(core_of, turn_x(d), 0)

    def col_sum(c, p):
        return runs[index[end_c, c], lines(p), :] * index[has_c, c].astype(F32)

    def paired(p, d, i):
        return col_sum(chunk(core, d) + i, p) + core_recv[p, turn_x(d) * nz + i].astype(F32)

    lower, upper = pl.ds(0, half), pl.ds(half, half)
    core_copies, far_copies, near_copies, quad_copies, pair_copies = {}, {}, {}, {}, {}

    def core_stage(p):
        for d in (2, 1, 3, 0):
            base, first = chunk(other, d), turn_x(d) * nz

            def fill(i, carry, base=base, first=first):
                core_send[p, first + i] = col_sum(base + i, p).astype(BF16)
                return carry

            lax.fori_loop(0, nz, fill, 0)
            blocks = pl.ds(first, nz)
            core_copies[p, d] = links.send(
                core_send.at[p, blocks], core_recv.at[p, blocks], to_core
            )

    def far_stage(p):
        core_copies[p, 2].wait_recv()

        def fill(i, carry):
            far_send[p, i] = paired(p, 2, i).astype(BF16)
            return carry

        lax.fori_loop(0, nz, fill, 0)
        far_copies[p, 0] = links.send(far_send.at[p, lower], far_recv.at[p, lower], to_x(1))
        far_copies[p, 1] = links.send(far_send.at[p, upper], far_recv.at[p, upper], to_x(NX - 1))

    def near_stage(p, way, with_far):
        d = (1, NX - 1)[way]
        if with_far:
            far_copies[p, way].wait_recv()
        else:
            core_copies[p, d].wait_recv()
        first = half * (way if with_far else 1 - way)

        def fill(i, carry):
            value = paired(p, d, i)
            if with_far:
                value = value + far_recv[p, i].astype(F32)
            near_send[p, way, i] = value.astype(BF16)
            return carry

        lax.fori_loop(first, first + half, fill, 0)
        blocks = pl.ds(first, half)
        near_copies[p, way, with_far] = links.send(
            near_send.at[p, way, blocks], near_recv.at[p, way, blocks], to_x(d)
        )

    def z_total(p, i):
        return (
            paired(p, 0, i) + near_recv[p, 0, i].astype(F32) + near_recv[p, 1, i].astype(F32)
        )

    def quad_stage(p):
        core_copies[p, 0].wait_recv()
        for way in range(2):
            for with_far in (False, True):
                near_copies[p, way, with_far].wait_recv()
        for e in mates:
            quad_send[p, e, 0] = z_total(p, zq * half + turn_zi(e)).astype(BF16)
            quad_send[p, e, 1] = z_total(p, (1 - zq) * half + turn_zi(e)).astype(BF16)
            quad_copies[p, e] = links.send(quad_send.at[p, e], quad_recv.at[p, e], to_mate(e))

    def pair_stage(p):
        value = z_total(p, pair_z)
        for e in mates:
            quad_copies[p, e].wait_recv()
            value = value + quad_recv[p, e, 1].astype(F32)
        pair_send[p] = value.astype(BF16)
        pair_copies[p] = links.send(pair_send.at[p], pair_recv.at[p], to_pair)

    def last_stage(p):
        value = z_total(p, z) + self_grad[lines(p), :]
        for e in mates:
            value = value + quad_recv[p, e, 0].astype(F32)
        pair_copies[p].wait_recv()
        return value + pair_recv[p].astype(F32)

    for p in range(parts):
        core_stage(p)
    far_stage(0)
    near_stage(0, 0, False)
    near_stage(0, 1, False)

    for copy in wz_copies:
        copy.wait_recv()
    w_part = wz_recv[0]
    for q in range(1, nz):
        w_part = w_part + wz_recv[q]
    wh_send[...] = w_part
    wh_copy = links.send(wh_send, wh_recv, to_zh)

    far_stage(1)
    near_stage(0, 0, True)
    near_stage(0, 1, True)
    near_stage(1, 0, False)
    near_stage(1, 1, False)

    wh_copy.wait_recv()
    w_part = w_part + wh_recv[...]
    wx_recv[x] = w_part
    wx_copies = [links.send(wx_recv.at[x], wx_recv.at[x], to_x(d)) for d in (2, 1, 3)]

    near_stage(1, 0, True)
    near_stage(1, 1, True)
    quad_stage(0)

    for copy in wx_copies:
        copy.wait_recv()
    w_part = wx_recv[0]
    for q in range(1, NX):
        w_part = w_part + wx_recv[q]
    wc_send[...] = w_part
    wc_copy = links.send(wc_send, wc_recv, to_core)

    pair_stage(0)
    quad_stage(1)

    wc_copy.wait_recv()
    w_part = w_part + wc_recv[...]
    gbias_ref[...] = jnp.concatenate(
        [w_part[part : part + 1], w_part[part + 1 : part + 2]], axis=1
    )
    store(gbias_ref, gbias_hbm)
    rows_here = pl.ds(pl.multiple_of(z * part, part), part)
    w_out[y, rows_here] = w_part[:part]
    gz_copies = [
        links.send(w_out.at[y, rows_here], w_out.at[y, rows_here], to_z(d)) for d in range(1, nz)
    ]

    pair_stage(1)
    for copy in gz_copies:
        copy.wait_recv()
    gy_copies = [links.send(w_out.at[y], w_out.at[y], to_y(d)) for d in (2, 1, 3)]
    grad = jnp.concatenate([last_stage(p) for p in range(parts)], axis=0)
    ingrad_ref[...] = jnp.transpose(grad).astype(BF16)
    store(ingrad_ref, ingrad_hbm)

    for copy in gy_copies:
        copy.wait_recv()
    gself_ref[:, :BLK] = w_out[0]
    gself_ref[:, BLK:] = w_out[1]
    gneigh_ref[:, :BLK] = w_out[2]
    gneigh_ref[:, BLK:] = w_out[3]
    store(gself_ref, gself_hbm)
    store(gneigh_ref, gneigh_hbm)
    links.finish()
    for copy in stores:
        copy.wait()


def place(*refs):
    count = len(refs) // 2
    copies = [
        pltpu.make_async_copy(refs[i], refs[count + i], refs[-1].at[i]) for i in range(count)
    ]
    for copy in copies:
        copy.start()
    for copy in copies:
        copy.wait()


def body(
    node_features,
    tile_values,
    tile_rows,
    tile_cols,
    weight_self,
    weight_neighbour,
    node_bias,
    output_grad,
):
    nz = lax.axis_size("row") // (NX * NC)
    half = nz // 2
    n_cols, n_rows = nz * NX * NC, lax.axis_size("col")
    tiles = tile_values.shape[2]
    feat, units = weight_self.shape
    hbm = pl.BlockSpec(memory_space=pltpu.HBM)
    block = (BLK, BLK)
    lines = (2, BLK // 2, BLK)
    part = BLK // nz + 8
    sems = 256
    results = (
        jax.ShapeDtypeStruct((BLK, units), BF16),
        jax.ShapeDtypeStruct((BLK, feat), BF16),
        jax.ShapeDtypeStruct((feat, units), F32),
        jax.ShapeDtypeStruct((feat, units), F32),
        jax.ShapeDtypeStruct((1, units), F32),
    )

    def halves(*lead):
        return pltpu.VMEM((2,) + lead + (BLK // 2, BLK), BF16)

    outs = pl.pallas_call(
        functools.partial(kernel, nz, tiles),
        out_shape=results,
        in_specs=[hbm] * 8,
        out_specs=(hbm,) * 5,
        scratch_shapes=[
            *(pltpu.VMEM(result.shape, result.dtype) for result in results),
            pltpu.VMEM((feat, units), BF16),
            pltpu.VMEM((feat, units), BF16),
            pltpu.VMEM((1, units), F32),
            pltpu.VMEM((BLK, units), BF16),
            pltpu.VMEM((1, tiles), jnp.int32),
            pltpu.VMEM((1, tiles), jnp.int32),
            pltpu.VMEM((16, BLK), jnp.int32),
            pltpu.SMEM((16, BLK), jnp.int32),
            pltpu.VMEM((tiles,) + block, BF16),
            pltpu.VMEM((n_cols,) + block, BF16),
            pltpu.VMEM((tiles,) + block, F32),
            pltpu.VMEM((BLK, units), F32),
            pltpu.VMEM(block, F32),
            halves(3, 2),
            halves(3, 2),
            halves(),
            halves(),
            pltpu.VMEM((n_rows,) + block, BF16),
            halves(NX * nz),
            halves(NX * nz),
            halves(nz),
            halves(nz),
            halves(2, nz),
            halves(2, nz),
            halves(half, 2),
            halves(half, 2),
            halves(),
            halves(),
            pltpu.VMEM((4, BLK + 16, BLK), BF16),
            pltpu.VMEM((4, BLK + 16, BLK), BF16),
            pltpu.VMEM((nz, part, BLK), F32),
            pltpu.VMEM((nz, part, BLK), F32),
            pltpu.VMEM((part, BLK), F32),
            pltpu.VMEM((part, BLK), F32),
            pltpu.VMEM((NX, part, BLK), F32),
            pltpu.VMEM((part, BLK), F32),
            pltpu.VMEM((part, BLK), F32),
            pltpu.VMEM((4,) + block, F32),
            pltpu.SemaphoreType.DMA((9,)),
            pltpu.SemaphoreType.DMA((5,)),
            pltpu.SemaphoreType.DMA((sems,)),
            pltpu.SemaphoreType.DMA((sems,)),
        ],
        compiler_params=pltpu.CompilerParams(
            collective_id=0, has_side_effects=True, vmem_limit_bytes=VMEM_LIMIT
        ),
        cost_estimate=pl.CostEstimate(
            flops=4 * tiles * BLK**3, bytes_accessed=2 * tiles * BLK**2, transcendentals=BLK * units
        ),
    )(
        node_features,
        weight_self,
        weight_neighbour,
        node_bias.reshape(1, units),
        output_grad,
        tile_rows.reshape(1, tiles),
        tile_cols.reshape(1, tiles),
        tile_values,
    )
    outs = pl.pallas_call(
        place,
        out_shape=results,
        in_specs=[hbm] * 5,
        out_specs=(hbm,) * 5,
        scratch_shapes=[pltpu.SemaphoreType.DMA((5,))],
        compiler_params=pltpu.CompilerParams(vmem_limit_bytes=VMEM_LIMIT),
    )(*outs)
    return (*outs[:4], outs[4].reshape(units))


def solution(mesh):
    placed = (
        P(("row", "col"), None),
        P("row", "col", None, None, None),
        P("row", "col", None),
        P("row", "col", None),
        P(),
        P(),
        P(),
        P(("row", "col"), None),
    )
    return jax.shard_map(
        body,
        mesh=mesh,
        in_specs=placed,
        out_specs=(P(("row", "col"), None), P(("row", "col"), None), P(), P(), P()),
        check_vma=False,
    )
```

time: 1190 us -> 118 us (0.10)
  waiting for transfers between devices: 927 us -> 0 us
  blocking collectives: 179 us -> 0 us
  Pallas kernels: 0 us -> 117 us
  local copies, waits for them, and re-layouts: 28.4 us -> 0 us
  matrix products: 24.2 us -> 0 us
  between operations: 13.9 us -> 0.64 us
    reduce_scatter x1 -> x0, waiting for transfers between devices: 440 us -> none  [body(): lax.psum_scatter(column_terms, 'row', scatter_dimension=0, tiled=True)]
    psum x1 -> x0, waiting for transfers between devices: 344 us -> none  [body(): lax.psum((jnp.sum(pre_grad.astype(jnp.float32), axis=0), inner_rows(node_...]
    all_gather x1 -> x0, waiting for transfers between devices: 126 us -> none  [body(): panels = lax.all_gather(node_features, 'row', axis=0, tiled=True)]
    pallas_call x0 -> x2, Pallas kernels: none -> 117 us  [the longest x1 105 us: body(): pl.pallas_call(functools.partial(kernel, nz, tiles), out_shape=results, i...]
    psum x1 -> x0, blocking collectives: 116 us -> none  [body(): lax.psum((jnp.sum(pre_grad.astype(jnp.float32), axis=0), inner_rows(node_...]
    all_gather x1 -> x0, blocking collectives: 63.3 us -> none  [body(): shard_grad = lax.all_gather(sum_grad, 'col', axis=0, tiled=True)]
    dot_general x10 -> x0, matrix products: 24.2 us -> none  [the longest x1 7.84 us: collect_tiles(): jnp.einsum('tij,tjf->tif', tile_block, picked, preferred_element_type=jnp...]
    dot_general x4 -> x0, local copies, waits for them, and re-layouts: 17.8 us -> none  [the longest x1 6.26 us: collect_tiles(): jnp.einsum('tij,tjf->tif', tile_block, picked, preferred_element_type=jnp...]
  transfers between devices with their start and end apart: 4 -> 0, of which waited for: 4 -> 0; matrix products, arithmetic and copies ran while one was open for 1% -> 0% of each run, Pallas kernels for 0% -> 0%
where the time goes in v1:
time: 118 us
  Pallas kernels  117 us (99%)
    pallas_call x1, Pallas kernels, body(): pl.pallas_call(functools.partial(kernel, nz, tiles), out_shape=results, i...  105 us
    pallas_call x1, Pallas kernels, body(): pl.pallas_call(place, out_shape=results, in_specs=[hbm] * 5, out_specs=(h...  12.1 us

profile of v1, /device:TPU:24, one launch (start us, length us, event | category | flops | bytes accessed | tf_op | source)
XLA Modules:
  0.0 117.7 jit_solution(14922627315781522023)
XLA Ops:
  0.6 104.9 %shard_map.119 = (bf16[128,256]{1,0:T(8,128)(2,1)}, bf16[128,128]{1,0:T(8,128)(2,1)}, f32[128,256]{1,0:T(8,128)}, f32[128,256]{1,0:T(8,128)}, f32[1,256]{1,0:T(1,128)}) custom-call(bf16[128,128]{1,0:T(8,128)(2,1)} %x_hbm.1, bf16[128,256]{1,0:T(8,128)(2,1)} %ws_hbm.1, bf16[128,256]{1,0:T(8,128)(2,1)} %wn_hbm.1, f32[1,256]{1,0:T(1,128)} %bitcast.4, ...), custom_call_target="tpu_custom_call" | custom-call | flops 939524096 | bytes 3670016 | tf_op jit(solution)/shard_map/pallas_call | solution.py:625
  105.6 12.1 %shard_map.120 = (bf16[128,256]{1,0:T(8,128)(2,1)}, bf16[128,128]{1,0:T(8,128)(2,1)}, f32[128,256]{1,0:T(8,128)}, f32[128,256]{1,0:T(8,128)}, f32[1,256]{1,0:T(1,128)}) custom-call(bf16[128,256]{1,0:T(8,128)(2,1)} %get-tuple-element.15.refs_0_, bf16[128,128]{1,0:T(8,128)(2,1)} %get-tuple-element.16.refs_1_, f32[128,256]{1,0:T(8,128)} %get-tuple-element.17.refs_2_, ...), custom_call_target="tpu_custom_call" | custom-call | tf_op jit(solution)/shard_map/pallas_call | solution.py:691

commit v2 on v1

--- a/solution.py
+++ b/solution.py
@@ -31,7 +31,7 @@
 
 class Links:
     def __init__(self, send_sems, recv_sems):
-        self.send_sems, self.recv_sems, self.copies = send_sems, recv_sems, []
+        self.send_sems, self.recv_sems, self.copies, self.sent = send_sems, recv_sems, [], 0
 
     def send(self, src, dst, device_id):
         at = len(self.copies)
@@ -47,9 +47,11 @@
         self.copies.append(copy)
         return copy
 
-    def finish(self):
-        for copy in self.copies:
+    def finish(self, upto=None):
+        upto = len(self.copies) if upto is None else upto
+        for copy in self.copies[self.sent : upto]:
             copy.wait_send()
+        self.sent = max(self.sent, upto)
 
 
 def send_sorted(block, carried, n_blocks, index, at):
@@ -78,8 +80,7 @@
     ids = lax.broadcasted_iota(jnp.int32, (tiles, n_blocks), 1)
     up_to = jnp.sum((block_down <= ids).astype(jnp.int32), axis=0, keepdims=True)
     held = jnp.sum((block_down == ids).astype(jnp.int32), axis=0, keepdims=True)
-    index[at + 3 : at + 4, :n_blocks] = jnp.maximum(up_to - 1, 0)
-    index[at + 4 : at + 5, :n_blocks] = jnp.minimum(held, 1)
+    index[at + 3 : at + 4, :n_blocks] = jnp.where(held > 0, up_to - 1, tiles)
 
 
 def kernel(
@@ -107,6 +108,7 @@
     wn_ref,
     bias_ref,
     og_ref,
+    x_their,
     rows_ref,
     cols_ref,
     index_buf,
@@ -196,7 +198,7 @@
     mates = [e for e in (1, half - 1) if e] + list(range(2, half - 1))
     mates = list(dict.fromkeys(mates))
 
-    ord_r, pan, keep_r, end_r, has_r, ord_c, grow, keep_c, end_c, has_c = range(10)
+    ord_r, pan, keep_r, end_r, ord_c, grow, keep_c, end_c = range(8)
 
     def slot(core_of, x_of, z_of):
         return (core_of * NX + x_of) * nz + z_of
@@ -211,7 +213,7 @@
         (bias_hbm, bias_ref),
         (tiles_hbm.at[0, 0], tile_buf),
         (wn_hbm, wn_ref),
-        (og_hbm, og_ref),
+        (og_hbm, og_ref.at[0]),
     ):
         loads.append(pltpu.make_async_copy(src, dst, load_sems.at[len(loads)]))
         loads[-1].start()
@@ -287,12 +289,13 @@
         cols = cols_ref[...]
         slots = slot(cols & (NC - 1), (cols // NC) & (NX - 1), cols // (NC * NX))
         send_sorted(rows, slots, n_rows, index_buf, 0)
-        send_sorted(slots, rows, n_cols, index_buf, 5)
+        send_sorted(slots, (rows & (NY - 1)) * 2 + rows // NY, n_cols, index_buf, 4)
+        runs[tiles] = jnp.zeros((BLK, BLK), F32)
         index_copy = pltpu.make_async_copy(index_buf, index, load_sems.at[len(loads)])
         index_copy.start()
         load_ws.wait()
         load_bias.wait()
-        self_pre[...] = dot_nn(panels[own], ws_ref[...]) + bias_ref[...]
+        self_pre[0] = dot_nn(panels[own], ws_ref[...]) + bias_ref[...]
         index_copy.wait()
 
     for i in range(nz + 2):
@@ -300,15 +303,19 @@
             own_step(i)
         if i == 0:
             prepare()
+        if i == nz - 1:
+            load_og.wait()
+            x_copy = links.send(panels.at[own], x_their, to_zh)
+            og_copy = links.send(og_ref.at[0], og_ref.at[1], to_zh)
         if 0 <= i - 1 < nz:
             near_step(i - 1)
         if 0 <= i - 2 < nz:
             far_step(i - 2)
     load_tiles.wait()
     load_wn.wait()
-    load_og.wait()
     for copy in crossed:
         copy.wait_recv()
+    gathered = len(links.copies)
 
     step = 8
 
@@ -329,7 +336,7 @@
         return slice(p * width, (p + 1) * width)
 
     def row_sum(r, p):
-        return runs[index[end_r, r], lines(p), :] * index[has_r, r].astype(F32)
+        return runs[index[end_r, r], lines(p), :]
 
     y_copies, zh_copies = {}, {}
     for p in range(parts):
@@ -337,38 +344,40 @@
             for h in range(2):
                 y_send[p, d - 1, h] = row_sum(h * NY + turn_y(d), p).astype(BF16)
             y_copies[p, d] = links.send(y_send.at[p, d - 1], y_recv.at[p, d - 1], to_y(d))
+    x_copy.wait_recv()
+    self_pre[1] = dot_nn(x_their[...], ws_ref[...]) + bias_ref[...]
+    og_copy.wait_recv()
+    links.finish(gathered)
+    sides = (zh, 1 - zh)
+    totals = {}
     for p in range(parts):
-        theirs = row_sum((1 - zh) * NY + y, p)
         for d in (1, 3, 2):
             y_copies[p, d].wait_recv()
-            theirs = theirs + y_recv[p, d - 1, 1 - zh].astype(F32)
-        zh_send[p] = theirs.astype(BF16)
+        for k, h in enumerate(sides):
+            value = row_sum(h * NY + y, p)
+            for d in (1, 3, 2):
+                value = value + y_recv[p, d - 1, h].astype(F32)
+            totals[k, p] = value
+            zh_send[p, h] = value.astype(BF16)
         zh_copies[p] = links.send(zh_send.at[p], zh_recv.at[p], to_zh)
-    mine = []
-    for p in range(parts):
-        total_here = row_sum(zh * NY + y, p)
-        for d in (1, 3, 2):
-            total_here = total_here + y_recv[p, d - 1, zh].astype(F32)
-        mine.append(total_here)
     for p in range(parts):
         zh_copies[p].wait_recv()
-        mine[p] = (mine[p] + zh_recv[p].astype(F32)).astype(BF16)
-    sums = jnp.concatenate(mine, axis=0)
-
-    pre = self_pre[...] + dot_nn(sums, wn_ref[...])
-    sig = 1.0 / (1.0 + jnp.exp(-pre))
-    pre_grad = (og_ref[...].astype(F32) * sig * (1.0 + pre * (1.0 - sig))).astype(BF16)
-
-    me = zh * NY + y
-    they = (1 - zh) * NY + y
-    gt[me] = dot_nt(wn_ref[...], pre_grad).astype(BF16)
-
-    def gt_part(r, p):
-        return gt.at[r, pl.ds(p * width, width)]
-
-    zh_gt = [links.send(gt_part(me, p), gt_part(me, p), to_zh) for p in range(parts)]
-    gt_copies = [links.send(gt.at[me], gt.at[me], to_y(d)) for d in (2, 1, 3)]
-    out_ref[...] = (pre * sig).astype(BF16)
+        for k, h in enumerate(sides):
+            totals[k, p] = (totals[k, p] + zh_recv[p, h].astype(F32)).astype(BF16)
+
+    def layer(k):
+        sums = jnp.concatenate([totals[k, p] for p in range(parts)], axis=0)
+        pre = self_pre[k] + dot_nn(sums, wn_ref[...])
+        sig = 1.0 / (1.0 + jnp.exp(-pre))
+        slope = sig * (1.0 + pre * (1.0 - sig))
+        return sums, pre * sig, (og_ref[k].astype(F32) * slope).astype(BF16)
+
+    sums, activated, pre_grad = layer(0)
+    gt[y * 2 + zh] = dot_nt(wn_ref[...], pre_grad).astype(BF16)
+    gt[y * 2 + 1 - zh] = dot_nt(wn_ref[...], layer(1)[2]).astype(BF16)
+    gt_here = gt.at[pl.ds(y * 2, 2)]
+    gt_copies = [links.send(gt_here, gt_here, to_y(d)) for d in (2, 1, 3)]
+    out_ref[...] = activated.astype(BF16)
     store(out_ref, out_hbm)
     self_grad[...] = dot_nt(ws_ref[...], pre_grad)
 
@@ -387,10 +396,8 @@
         wy_send[q, BLK:] = bias_rows
     wy_recv[y] = wy_send[y]
 
-    for p in range(parts):
-        zh_gt[p].wait_recv()
-        gt_copies += [links.send(gt_part(they, p), gt_part(they, p), to_y(d)) for d in (2, 1, 3)]
     wy_copies = [links.send(wy_send.at[turn_y(d)], wy_recv.at[y], to_y(d)) for d in (2, 1, 3)]
+    links.finish(len(links.copies) - 6)
     for copy in gt_copies:
         copy.wait_recv()
 
@@ -423,7 +430,7 @@
         return slot(core_of, turn_x(d), 0)
 
     def col_sum(c, p):
-        return runs[index[end_c, c], lines(p), :] * index[has_c, c].astype(F32)
+        return runs[index[end_c, c], lines(p), :]
 
     def paired(p, d, i):
         return col_sum(chunk(core, d) + i, p) + core_recv[p, turn_x(d) * nz + i].astype(F32)
@@ -434,12 +441,8 @@
     def core_stage(p):
         for d in (2, 1, 3, 0):
             base, first = chunk(other, d), turn_x(d) * nz
-
-            def fill(i, carry, base=base, first=first):
+            for i in range(nz):
                 core_send[p, first + i] = col_sum(base + i, p).astype(BF16)
-                return carry
-
-            lax.fori_loop(0, nz, fill, 0)
             blocks = pl.ds(first, nz)
             core_copies[p, d] = links.send(
                 core_send.at[p, blocks], core_recv.at[p, blocks], to_core
@@ -447,12 +450,8 @@
 
     def far_stage(p):
         core_copies[p, 2].wait_recv()
-
-        def fill(i, carry):
+        for i in range(nz):
             far_send[p, i] = paired(p, 2, i).astype(BF16)
-            return carry
-
-        lax.fori_loop(0, nz, fill, 0)
         far_copies[p, 0] = links.send(far_send.at[p, lower], far_recv.at[p, lower], to_x(1))
         far_copies[p, 1] = links.send(far_send.at[p, upper], far_recv.at[p, upper], to_x(NX - 1))
 
@@ -463,15 +462,11 @@
         else:
             core_copies[p, d].wait_recv()
         first = half * (way if with_far else 1 - way)
-
-        def fill(i, carry):
+        for i in range(first, first + half):
             value = paired(p, d, i)
             if with_far:
                 value = value + far_recv[p, i].astype(F32)
             near_send[p, way, i] = value.astype(BF16)
-            return carry
-
-        lax.fori_loop(first, first + half, fill, 0)
         blocks = pl.ds(first, half)
         near_copies[p, way, with_far] = links.send(
             near_send.at[p, way, blocks], near_recv.at[p, way, blocks], to_x(d)
@@ -560,6 +555,7 @@
     ]
 
     pair_stage(1)
+    links.finish(len(links.copies) - nz)
     for copy in gz_copies:
         copy.wait_recv()
     gy_copies = [links.send(w_out.at[y], w_out.at[y], to_y(d)) for d in (2, 1, 3)]
@@ -581,14 +577,23 @@
 
 
 def place(*refs):
-    count = len(refs) // 2
-    copies = [
-        pltpu.make_async_copy(refs[i], refs[count + i], refs[-1].at[i]) for i in range(count)
-    ]
-    for copy in copies:
-        copy.start()
-    for copy in copies:
-        copy.wait()
+    count = (len(refs) - 2) // 3
+    sources, targets, held = (refs[i * count : (i + 1) * count] for i in range(3))
+    ins, outs = refs[-2:]
+    moves = []
+    for i in range(count):
+        moves.append(
+            (
+                pltpu.make_async_copy(sources[i], held[i], ins.at[i]),
+                pltpu.make_async_copy(held[i], targets[i], outs.at[i]),
+            )
+        )
+        moves[-1][0].start()
+    for into, out in moves:
+        into.wait()
+        out.start()
+    for _, out in moves:
+        out.wait()
 
 
 def body(
@@ -632,20 +637,21 @@
             pltpu.VMEM((feat, units), BF16),
             pltpu.VMEM((feat, units), BF16),
             pltpu.VMEM((1, units), F32),
-            pltpu.VMEM((BLK, units), BF16),
+            pltpu.VMEM((2, BLK, units), BF16),
+            pltpu.VMEM((BLK, feat), BF16),
             pltpu.VMEM((1, tiles), jnp.int32),
             pltpu.VMEM((1, tiles), jnp.int32),
             pltpu.VMEM((16, BLK), jnp.int32),
             pltpu.SMEM((16, BLK), jnp.int32),
             pltpu.VMEM((tiles,) + block, BF16),
             pltpu.VMEM((n_cols,) + block, BF16),
-            pltpu.VMEM((tiles,) + block, F32),
-            pltpu.VMEM((BLK, units), F32),
+            pltpu.VMEM((tiles + 1,) + block, F32),
+            pltpu.VMEM((2, BLK, units), F32),
             pltpu.VMEM(block, F32),
             halves(3, 2),
             halves(3, 2),
-            halves(),
-            halves(),
+            halves(2),
+            halves(2),
             pltpu.VMEM((n_rows,) + block, BF16),
             halves(NX * nz),
             halves(NX * nz),
@@ -693,7 +699,11 @@
         out_shape=results,
         in_specs=[hbm] * 5,
         out_specs=(hbm,) * 5,
-        scratch_shapes=[pltpu.SemaphoreType.DMA((5,))],
+        scratch_shapes=[
+            *(pltpu.VMEM(result.shape, result.dtype) for result in results),
+            pltpu.SemaphoreType.DMA((5,)),
+            pltpu.SemaphoreType.DMA((5,)),
+        ],
         compiler_params=pltpu.CompilerParams(vmem_limit_bytes=VMEM_LIMIT),
     )(*outs)
     return (*outs[:4], outs[4].reshape(units))

time: 118 us -> 106 us (0.90)
  Pallas kernels: 117 us -> 105 us
    pallas_call x1, Pallas kernels: 12.1 us -> 1.77 us  [body(): pl.pallas_call(place, out_shape=results, in_specs=[hbm] * 5, out_specs=(h...]
    pallas_call x1, Pallas kernels: 105 us -> 103 us  [body(): pl.pallas_call(functools.partial(kernel, nz, tiles), out_shape=results, i...]
where the time goes in v2:
time: 106 us; the launch traced here: 105 us
  Pallas kernels  105 us (99%)
    pallas_call x1, Pallas kernels, body(): pl.pallas_call(functools.partial(kernel, nz, tiles), out_shape=results, i...  103 us

profile of v2, /device:TPU:24, one launch (start us, length us, event | category | flops | bytes accessed | tf_op | source)
XLA Modules:
  0.0 105.3 jit_solution(17506469518482164560)
XLA Ops:
  0.6 102.9 %shard_map.119 = (bf16[128,256]{1,0:T(8,128)(2,1)}, bf16[128,128]{1,0:T(8,128)(2,1)}, f32[128,256]{1,0:T(8,128)}, f32[128,256]{1,0:T(8,128)}, f32[1,256]{1,0:T(1,128)}) custom-call(bf16[128,128]{1,0:T(8,128)(2,1)} %x_hbm.1, bf16[128,256]{1,0:T(8,128)(2,1)} %ws_hbm.1, bf16[128,256]{1,0:T(8,128)(2,1)} %wn_hbm.1, f32[1,256]{1,0:T(1,128)} %bitcast.4, ...), custom_call_target="tpu_custom_call" | custom-call | flops 939524096 | bytes 3670016 | tf_op jit(solution)/shard_map/pallas_call | solution.py:630
  103.6 1.8 %shard_map.120 = (bf16[128,256]{1,0:T(8,128)(2,1)}, bf16[128,128]{1,0:T(8,128)(2,1)}, f32[128,256]{1,0:T(8,128)}, f32[128,256]{1,0:T(8,128)}, f32[1,256]{1,0:T(1,128)}) custom-call(bf16[128,256]{1,0:T(8,128)(2,1)} %get-tuple-element.15.refs_0_, bf16[128,128]{1,0:T(8,128)(2,1)} %get-tuple-element.16.refs_1_, f32[128,256]{1,0:T(8,128)} %get-tuple-element.17.refs_2_, ...), custom_call_target="tpu_custom_call" | custom-call | tf_op jit(solution)/shard_map/pallas_call | solution.py:697

commit v3 on v2

--- a/solution.py
+++ b/solution.py
@@ -54,33 +54,69 @@
         self.sent = max(self.sent, upto)
 
 
-def send_sorted(block, carried, n_blocks, index, at):
+def iota(shape, axis):
+    return lax.broadcasted_iota(jnp.int32, shape, axis)
+
+
+def turned(line):
+    n = line.shape[1]
+    diagonal = iota((n, n), 0) == iota((n, n), 1)
+    return jnp.sum(jnp.where(diagonal, line, 0), axis=1, keepdims=True)
+
+
+def laid(column):
+    n = column.shape[0]
+    diagonal = iota((n, n), 0) == iota((n, n), 1)
+    return jnp.sum(jnp.where(diagonal, column, 0), axis=0, keepdims=True)
+
+
+def order_pairs(block, carried, gate, n_blocks, index, at):
+    tiles = block.shape[1]
+    places = tiles + n_blocks
+    shape = (tiles, tiles)
+    block_down = turned(block)
+    earlier = (block == block_down) & (iota(shape, 1) < iota(shape, 0))
+    rank = jnp.sum(earlier.astype(jnp.int32), axis=1, keepdims=True)
+    ids = iota((tiles, n_blocks), 1)
+    held = jnp.sum((block_down == ids).astype(jnp.int32), axis=0, keepdims=True)
+    padded = ((held + 1) // 2) * 2
+    base = jnp.sum(jnp.where(ids < block_down, padded, 0), axis=1, keepdims=True)
+    place = base + rank
+    hot = place == iota((tiles, places), 1)
+
+    def by_place(column):
+        return jnp.sum(jnp.where(hot, column, 0), axis=0, keepdims=True)
+
+    index[at : at + 1, :places] = tiles - by_place(tiles - iota((tiles, 1), 0))
+    index[at + 1 : at + 2, :places] = by_place(turned(carried))
+    index[at + 2 : at + 3, :places] = by_place(jnp.minimum(rank // 2, 1))
+    index[at + 3 : at + 4, :places] = by_place(gate(block_down))
+    small = (n_blocks, n_blocks)
+    up_to = jnp.where(iota(small, 0) <= iota(small, 1), turned(padded), 0)
+    last = jnp.sum(up_to, axis=0, keepdims=True) // 2 - 1
+    index[at + 4 : at + 5, :n_blocks] = jnp.where(held > 0, last, tiles)
+    return laid(place)
+
+
+def order_tiles(block, carried, n_blocks, index, at):
     tiles = block.shape[1]
     shape = (tiles, tiles)
-    down = lax.broadcasted_iota(jnp.int32, shape, 0)
-    across = lax.broadcasted_iota(jnp.int32, shape, 1)
-
-    def turned(line):
-        return jnp.sum(jnp.where(down == across, line, 0), axis=1, keepdims=True)
-
-    block_down, carried_down = turned(block), turned(carried)
-    before = (block < block_down) | ((block == block_down) & (across < down))
-    rank = jnp.sum(before.astype(jnp.int32), axis=1, keepdims=True)
-    goes_on = jnp.sum(
-        ((block == block_down) & (across < down)).astype(jnp.int32), axis=1, keepdims=True
-    )
-    hot = rank == across
-
-    def sorted_line(values):
-        return jnp.sum(jnp.where(hot, values, 0), axis=0, keepdims=True)
-
-    index[at : at + 1, :tiles] = sorted_line(down)
-    index[at + 1 : at + 2, :tiles] = sorted_line(carried_down)
-    index[at + 2 : at + 3, :tiles] = sorted_line(jnp.minimum(goes_on, 1))
-    ids = lax.broadcasted_iota(jnp.int32, (tiles, n_blocks), 1)
+    block_down = turned(block)
+    earlier = (block == block_down) & (iota(shape, 1) < iota(shape, 0))
+    before = (block < block_down) | earlier
+    place = jnp.sum(before.astype(jnp.int32), axis=1, keepdims=True)
+    rank = jnp.sum(earlier.astype(jnp.int32), axis=1, keepdims=True)
+    hot = place == iota(shape, 1)
+
+    def by_place(column):
+        return jnp.sum(jnp.where(hot, column, 0), axis=0, keepdims=True)
+
+    index[at : at + 1, :tiles] = by_place(turned(carried))
+    index[at + 1 : at + 2, :tiles] = by_place(jnp.minimum(rank, 1))
+    ids = iota((tiles, n_blocks), 1)
     up_to = jnp.sum((block_down <= ids).astype(jnp.int32), axis=0, keepdims=True)
     held = jnp.sum((block_down == ids).astype(jnp.int32), axis=0, keepdims=True)
-    index[at + 3 : at + 4, :n_blocks] = jnp.where(held > 0, up_to - 1, tiles)
+    index[at + 2 : at + 3, :n_blocks] = jnp.where(held > 0, up_to - 1, tiles)
 
 
 def kernel(
@@ -116,6 +152,7 @@
     tile_buf,
     panels,
     runs,
+    products,
     self_pre,
     self_grad,
     y_send,
@@ -198,7 +235,7 @@
     mates = [e for e in (1, half - 1) if e] + list(range(2, half - 1))
     mates = list(dict.fromkeys(mates))
 
-    ord_r, pan, keep_r, end_r, ord_c, grow, keep_c, end_c = range(8)
+    ord_r, pan, keep_r, grow, end_r, made, keep_c, end_c = range(8)
 
     def slot(core_of, x_of, z_of):
         return (core_of * NX + x_of) * nz + z_of
@@ -211,7 +248,7 @@
         (cols_hbm, cols_ref),
         (ws_hbm, ws_ref),
         (bias_hbm, bias_ref),
-        (tiles_hbm.at[0, 0], tile_buf),
+        (tiles_hbm.at[0, 0], tile_buf.at[pl.ds(0, tiles)]),
         (wn_hbm, wn_ref),
         (og_hbm, og_ref.at[0]),
     ):
@@ -288,9 +325,12 @@
         rows = rows_ref[...]
         cols = cols_ref[...]
         slots = slot(cols & (NC - 1), (cols // NC) & (NX - 1), cols // (NC * NX))
-        send_sorted(rows, slots, n_rows, index_buf, 0)
-        send_sorted(slots, (rows & (NY - 1)) * 2 + rows // NY, n_cols, index_buf, 4)
+        place = order_pairs(
+            rows, slots, lambda r: (r & (NY - 1)) * 2 + r // NY, n_rows, index_buf, 0
+        )
+        order_tiles(slots, place, n_cols, index_buf, 5)
         runs[tiles] = jnp.zeros((BLK, BLK), F32)
+        tile_buf[tiles] = jnp.zeros((BLK, BLK), BF16)
         index_copy = pltpu.make_async_copy(index_buf, index, load_sems.at[len(loads)])
         index_copy.start()
         load_ws.wait()
@@ -317,17 +357,20 @@
         copy.wait_recv()
     gathered = len(links.copies)
 
-    step = 8
+    n_pairs = (tiles + n_rows) // 2
+    step = 4
 
     def collect(k, acc):
         for u in range(step):
             n = k * step + u
-            term = dot_nn(tile_buf[index[ord_r, n]], panels[index[pan, n]])
-            acc = acc * index[keep_r, n].astype(F32) + term
+            here = [2 * n, 2 * n + 1]
+            left = jnp.concatenate([tile_buf[index[ord_r, i]] for i in here], axis=1)
+            right = jnp.concatenate([panels[index[pan, i]] for i in here], axis=0)
+            acc = acc * index[keep_r, 2 * n].astype(F32) + dot_nn(left, right)
             runs[n] = acc
         return acc
 
-    lax.fori_loop(0, tiles // step, collect, jnp.zeros((BLK, BLK), F32))
+    lax.fori_loop(0, n_pairs // step, collect, jnp.zeros((BLK, BLK), F32))
 
     parts = 2
     width = BLK // parts
@@ -401,16 +444,30 @@
     for copy in gt_copies:
         copy.wait_recv()
 
-    def spread(k, acc):
+    def spread(k, carry):
         for u in range(step):
             n = k * step + u
-            term = dot_nn(gt[index[grow, n]], tile_buf[index[ord_c, n]])
-            acc = acc * index[keep_c, n].astype(F32) + term
-            runs[n] = acc
-        return acc
-
-    steps = tiles // step
-    acc = lax.fori_loop(0, steps // 2, spread, jnp.zeros((BLK, BLK), F32))
+            right = jnp.concatenate(
+                [tile_buf[index[ord_r, 2 * n]], tile_buf[index[ord_r, 2 * n + 1]]], axis=1
+            )
+            terms = dot_nn(gt[index[grow, 2 * n]], right)
+            products[2 * n] = terms[:, :BLK]
+            products[2 * n + 1] = terms[:, BLK:]
+        return carry
+
+    def add_up(p):
+        def add(k, acc):
+            for u in range(8):
+                n = k * 8 + u
+                term = products[index[made, n], lines(p), :]
+                acc = acc * index[keep_c, n].astype(F32) + term
+                runs[n, lines(p), :] = acc
+            return acc
+
+        lax.fori_loop(0, tiles // 8, add, jnp.zeros((width, BLK), F32))
+
+    steps = n_pairs // step
+    lax.fori_loop(0, steps // 2, spread, 0)
 
     for copy in wy_copies:
         copy.wait_recv()
@@ -424,7 +481,7 @@
     wz_recv[z] = wz_send[z]
     wz_copies = [links.send(wz_send.at[turn_z(d)], wz_recv.at[z], to_z(d)) for d in range(1, nz)]
 
-    lax.fori_loop(steps // 2, steps, spread, acc)
+    lax.fori_loop(steps // 2, steps, spread, 0)
 
     def chunk(core_of, d):
         return slot(core_of, turn_x(d), 0)
@@ -502,11 +559,8 @@
         pair_copies[p].wait_recv()
         return value + pair_recv[p].astype(F32)
 
-    for p in range(parts):
-        core_stage(p)
-    far_stage(0)
-    near_stage(0, 0, False)
-    near_stage(0, 1, False)
+    add_up(0)
+    core_stage(0)
 
     for copy in wz_copies:
         copy.wait_recv()
@@ -516,20 +570,20 @@
     wh_send[...] = w_part
     wh_copy = links.send(wh_send, wh_recv, to_zh)
 
-    far_stage(1)
-    near_stage(0, 0, True)
-    near_stage(0, 1, True)
-    near_stage(1, 0, False)
-    near_stage(1, 1, False)
+    add_up(1)
+    core_stage(1)
+    far_stage(0)
+    near_stage(0, 0, False)
+    near_stage(0, 1, False)
 
     wh_copy.wait_recv()
     w_part = w_part + wh_recv[...]
     wx_recv[x] = w_part
     wx_copies = [links.send(wx_recv.at[x], wx_recv.at[x], to_x(d)) for d in (2, 1, 3)]
 
-    near_stage(1, 0, True)
-    near_stage(1, 1, True)
-    quad_stage(0)
+    far_stage(1)
+    near_stage(0, 0, True)
+    near_stage(0, 1, True)
 
     for copy in wx_copies:
         copy.wait_recv()
@@ -539,8 +593,10 @@
     wc_send[...] = w_part
     wc_copy = links.send(wc_send, wc_recv, to_core)
 
-    pair_stage(0)
-    quad_stage(1)
+    near_stage(1, 0, False)
+    near_stage(1, 1, False)
+    near_stage(1, 0, True)
+    near_stage(1, 1, True)
 
     wc_copy.wait_recv()
     w_part = w_part + wc_recv[...]
@@ -554,11 +610,14 @@
         links.send(w_out.at[y, rows_here], w_out.at[y, rows_here], to_z(d)) for d in range(1, nz)
     ]
 
-    pair_stage(1)
-    links.finish(len(links.copies) - nz)
+    quad_stage(0)
     for copy in gz_copies:
         copy.wait_recv()
     gy_copies = [links.send(w_out.at[y], w_out.at[y], to_y(d)) for d in (2, 1, 3)]
+    pair_stage(0)
+    quad_stage(1)
+    pair_stage(1)
+    links.finish(len(links.copies) - nz)
     grad = jnp.concatenate([last_stage(p) for p in range(parts)], axis=0)
     ingrad_ref[...] = jnp.transpose(grad).astype(BF16)
     store(ingrad_ref, ingrad_hbm)
@@ -641,11 +700,12 @@
             pltpu.VMEM((BLK, feat), BF16),
             pltpu.VMEM((1, tiles), jnp.int32),
             pltpu.VMEM((1, tiles), jnp.int32),
-            pltpu.VMEM((16, BLK), jnp.int32),
-            pltpu.SMEM((16, BLK), jnp.int32),
-            pltpu.VMEM((tiles,) + block, BF16),
+            pltpu.VMEM((8, BLK), jnp.int32),
+            pltpu.SMEM((8, BLK), jnp.int32),
+            pltpu.VMEM((tiles + 1,) + block, BF16),
             pltpu.VMEM((n_cols,) + block, BF16),
             pltpu.VMEM((tiles + 1,) + block, F32),
+            pltpu.VMEM((tiles + n_rows,) + block, F32),
             pltpu.VMEM((2, BLK, units), F32),
             pltpu.VMEM(block, F32),
             halves(3, 2),

time: 106 us -> 110 us (1.038)
  Pallas kernels: 105 us -> 108 us
    pallas_call x1, Pallas kernels: 103 us -> 106 us  [body(): pl.pallas_call(functools.partial(kernel, nz, tiles), out_shape=results, i...]
where the time goes in v3:
time: 110 us; the launch traced here: 109 us
  Pallas kernels  108 us (98%)
    pallas_call x1, Pallas kernels, body(): pl.pallas_call(functools.partial(kernel, nz, tiles), out_shape=results, i...  106 us

profile of v3, /device:TPU:24, one launch (start us, length us, event | category | flops | bytes accessed | tf_op | source)
XLA Modules:
  0.0 108.9 jit_solution(8395817590801633865)
XLA Ops:
  0.6 106.5 %shard_map.119 = (bf16[128,256]{1,0:T(8,128)(2,1)}, bf16[128,128]{1,0:T(8,128)(2,1)}, f32[128,256]{1,0:T(8,128)}, f32[128,256]{1,0:T(8,128)}, f32[1,256]{1,0:T(1,128)}) custom-call(bf16[128,128]{1,0:T(8,128)(2,1)} %x_hbm.1, bf16[128,256]{1,0:T(8,128)(2,1)} %ws_hbm.1, bf16[128,256]{1,0:T(8,128)(2,1)} %wn_hbm.1, f32[1,256]{1,0:T(1,128)} %bitcast.4, ...), custom_call_target="tpu_custom_call" | custom-call | flops 939524096 | bytes 3670016 | tf_op jit(solution)/shard_map/pallas_call | solution.py:689
  107.1 1.8 %shard_map.120 = (bf16[128,256]{1,0:T(8,128)(2,1)}, bf16[128,128]{1,0:T(8,128)(2,1)}, f32[128,256]{1,0:T(8,128)}, f32[128,256]{1,0:T(8,128)}, f32[1,256]{1,0:T(1,128)}) custom-call(bf16[128,256]{1,0:T(8,128)(2,1)} %get-tuple-element.15.refs_0_, bf16[128,128]{1,0:T(8,128)(2,1)} %get-tuple-element.16.refs_1_, f32[128,256]{1,0:T(8,128)} %get-tuple-element.17.refs_2_, ...), custom_call_target="tpu_custom_call" | custom-call | tf_op jit(solution)/shard_map/pallas_call | solution.py:757

commit v4 on v2

--- a/solution.py
+++ b/solution.py
@@ -54,30 +54,59 @@
         self.sent = max(self.sent, upto)
 
 
-def send_sorted(block, carried, n_blocks, index, at):
+def iota(shape, axis):
+    return lax.broadcasted_iota(jnp.int32, shape, axis)
+
+
+def turned(line):
+    n = line.shape[1]
+    diagonal = iota((n, n), 0) == iota((n, n), 1)
+    return jnp.sum(jnp.where(diagonal, line, 0), axis=1, keepdims=True)
+
+
+def order_pairs(block, carried, n_blocks, index, at):
+    tiles = block.shape[1]
+    places = tiles + n_blocks
+    shape = (tiles, tiles)
+    block_down = turned(block)
+    earlier = (block == block_down) & (iota(shape, 1) < iota(shape, 0))
+    rank = jnp.sum(earlier.astype(jnp.int32), axis=1, keepdims=True)
+    ids = iota((tiles, n_blocks), 1)
+    held = jnp.sum((block_down == ids).astype(jnp.int32), axis=0, keepdims=True)
+    padded = ((held + 1) // 2) * 2
+    base = jnp.sum(jnp.where(ids < block_down, padded, 0), axis=1, keepdims=True)
+    place = base + rank
+    hot = place == iota((tiles, places), 1)
+
+    def by_place(column):
+        return jnp.sum(jnp.where(hot, column, 0), axis=0, keepdims=True)
+
+    index[at : at + 1, :places] = tiles - by_place(tiles - iota((tiles, 1), 0))
+    index[at + 1 : at + 2, :places] = by_place(turned(carried))
+    index[at + 2 : at + 3, :places] = by_place(jnp.minimum(rank // 2, 1))
+    small = (n_blocks, n_blocks)
+    up_to = jnp.where(iota(small, 0) <= iota(small, 1), turned(padded), 0)
+    last = jnp.sum(up_to, axis=0, keepdims=True) // 2 - 1
+    index[at + 3 : at + 4, :n_blocks] = jnp.where(held > 0, last, tiles)
+
+
+def order_tiles(block, carried, n_blocks, index, at):
     tiles = block.shape[1]
     shape = (tiles, tiles)
-    down = lax.broadcasted_iota(jnp.int32, shape, 0)
-    across = lax.broadcasted_iota(jnp.int32, shape, 1)
-
-    def turned(line):
-        return jnp.sum(jnp.where(down == across, line, 0), axis=1, keepdims=True)
-
-    block_down, carried_down = turned(block), turned(carried)
-    before = (block < block_down) | ((block == block_down) & (across < down))
-    rank = jnp.sum(before.astype(jnp.int32), axis=1, keepdims=True)
-    goes_on = jnp.sum(
-        ((block == block_down) & (across < down)).astype(jnp.int32), axis=1, keepdims=True
-    )
-    hot = rank == across
-
-    def sorted_line(values):
-        return jnp.sum(jnp.where(hot, values, 0), axis=0, keepdims=True)
-
-    index[at : at + 1, :tiles] = sorted_line(down)
-    index[at + 1 : at + 2, :tiles] = sorted_line(carried_down)
-    index[at + 2 : at + 3, :tiles] = sorted_line(jnp.minimum(goes_on, 1))
-    ids = lax.broadcasted_iota(jnp.int32, (tiles, n_blocks), 1)
+    block_down = turned(block)
+    earlier = (block == block_down) & (iota(shape, 1) < iota(shape, 0))
+    before = (block < block_down) | earlier
+    place = jnp.sum(before.astype(jnp.int32), axis=1, keepdims=True)
+    rank = jnp.sum(earlier.astype(jnp.int32), axis=1, keepdims=True)
+    hot = place == iota(shape, 1)
+
+    def by_place(column):
+        return jnp.sum(jnp.where(hot, column, 0), axis=0, keepdims=True)
+
+    index[at : at + 1, :tiles] = by_place(iota((tiles, 1), 0))
+    index[at + 1 : at + 2, :tiles] = by_place(turned(carried))
+    index[at + 2 : at + 3, :tiles] = by_place(jnp.minimum(rank, 1))
+    ids = iota((tiles, n_blocks), 1)
     up_to = jnp.sum((block_down <= ids).astype(jnp.int32), axis=0, keepdims=True)
     held = jnp.sum((block_down == ids).astype(jnp.int32), axis=0, keepdims=True)
     index[at + 3 : at + 4, :n_blocks] = jnp.where(held > 0, up_to - 1, tiles)
@@ -107,8 +136,8 @@
     ws_ref,
     wn_ref,
     bias_ref,
-    og_ref,
-    x_their,
+    nodes,
+    nodes_relay,
     rows_ref,
     cols_ref,
     index_buf,
@@ -121,6 +150,7 @@
     y_send,
     y_recv,
     zh_send,
+    zh_relay,
     zh_recv,
     gt,
     core_send,
@@ -168,6 +198,12 @@
     def at_col(zh_to, y_to):
         return {"row": row, "col": zh_to * NY + y_to}
 
+    parts = 2
+    width = BLK // parts
+
+    def lines(p):
+        return pl.ds(p * width, width)
+
     def turn_z(d):
         return lax.rem(z + d, nz)
 
@@ -195,6 +231,13 @@
     to_pair = at_row((1 - zq) * half + zi, x, core)
     to_core = at_row(z, x, other)
     to_zh = at_col(1 - zh, y)
+
+    def along_z(d):
+        z_to = lax.rem(zh * nz + z + d, 2 * nz)
+        return {"row": (lax.rem(z_to, nz) * NX + x) * NC + core, "col": z_to // nz * NY + y}
+
+    first_leg = [along_z(nz - 1), along_z(nz + 1)]
+    last_leg = [along_z(1), along_z(2 * nz - 1)]
     mates = [e for e in (1, half - 1) if e] + list(range(2, half - 1))
     mates = list(dict.fromkeys(mates))
 
@@ -211,17 +254,19 @@
         (cols_hbm, cols_ref),
         (ws_hbm, ws_ref),
         (bias_hbm, bias_ref),
-        (tiles_hbm.at[0, 0], tile_buf),
+        (tiles_hbm.at[0, 0], tile_buf.at[pl.ds(0, tiles)]),
         (wn_hbm, wn_ref),
-        (og_hbm, og_ref.at[0]),
+        (x_hbm, nodes.at[0, :, pl.ds(0, BLK)]),
+        (og_hbm, nodes.at[0, :, pl.ds(BLK, 2 * BLK)]),
     ):
         loads.append(pltpu.make_async_copy(src, dst, load_sems.at[len(loads)]))
         loads[-1].start()
-    load_x, load_rows, load_cols, load_ws, load_bias, load_tiles, load_wn, load_og = loads
+    load_x, load_rows, load_cols, load_ws, load_bias, load_tiles, load_wn, load_own, load_og = loads
 
     barrier = pltpu.get_barrier_semaphore()
     partners = [to_z(d) for d in range(1, nz)] + [to_x(d) for d in range(1, NX)]
     partners += [to_y(d) for d in range(1, NY)] + [to_core, to_zh]
+    partners += first_leg + last_leg
     for partner in partners:
         pl.semaphore_signal(barrier, inc=1, device_id=partner, device_id_type=MESH)
     load_x.wait()
@@ -288,9 +333,10 @@
         rows = rows_ref[...]
         cols = cols_ref[...]
         slots = slot(cols & (NC - 1), (cols // NC) & (NX - 1), cols // (NC * NX))
-        send_sorted(rows, slots, n_rows, index_buf, 0)
-        send_sorted(slots, (rows & (NY - 1)) * 2 + rows // NY, n_cols, index_buf, 4)
+        order_pairs(rows, slots, n_rows, index_buf, 0)
+        order_tiles(slots, (rows & (NY - 1)) * 2 + rows // NY, n_cols, index_buf, 4)
         runs[tiles] = jnp.zeros((BLK, BLK), F32)
+        tile_buf[tiles] = jnp.zeros((BLK, BLK), BF16)
         index_copy = pltpu.make_async_copy(index_buf, index, load_sems.at[len(loads)])
         index_copy.start()
         load_ws.wait()
@@ -304,9 +350,12 @@
         if i == 0:
             prepare()
         if i == nz - 1:
+            load_own.wait()
             load_og.wait()
-            x_copy = links.send(panels.at[own], x_their, to_zh)
-            og_copy = links.send(og_ref.at[0], og_ref.at[1], to_zh)
+            own_copies = [
+                links.send(nodes.at[0, lines(p)], nodes_relay.at[lines(p)], first_leg[p])
+                for p in range(parts)
+            ]
         if 0 <= i - 1 < nz:
             near_step(i - 1)
         if 0 <= i - 2 < nz:
@@ -316,24 +365,26 @@
     for copy in crossed:
         copy.wait_recv()
     gathered = len(links.copies)
-
-    step = 8
+    for p in range(parts):
+        own_copies[p].wait_recv()
+        own_copies[p] = links.send(
+            nodes_relay.at[lines(p)], nodes.at[1, lines(p)], last_leg[p]
+        )
+
+    n_pairs = (tiles + n_rows) // 2
+    step = 4
 
     def collect(k, acc):
         for u in range(step):
             n = k * step + u
-            term = dot_nn(tile_buf[index[ord_r, n]], panels[index[pan, n]])
-            acc = acc * index[keep_r, n].astype(F32) + term
+            here = [2 * n, 2 * n + 1]
+            left = jnp.concatenate([tile_buf[index[ord_r, i]] for i in here], axis=1)
+            right = jnp.concatenate([panels[index[pan, i]] for i in here], axis=0)
+            acc = acc * index[keep_r, 2 * n].astype(F32) + dot_nn(left, right)
             runs[n] = acc
         return acc
 
-    lax.fori_loop(0, tiles // step, collect, jnp.zeros((BLK, BLK), F32))
-
-    parts = 2
-    width = BLK // parts
-
-    def lines(p):
-        return slice(p * width, (p + 1) * width)
+    lax.fori_loop(0, n_pairs // step, collect, jnp.zeros((BLK, BLK), F32))
 
     def row_sum(r, p):
         return runs[index[end_r, r], lines(p), :]
@@ -344,9 +395,9 @@
             for h in range(2):
                 y_send[p, d - 1, h] = row_sum(h * NY + turn_y(d), p).astype(BF16)
             y_copies[p, d] = links.send(y_send.at[p, d - 1], y_recv.at[p, d - 1], to_y(d))
-    x_copy.wait_recv()
-    self_pre[1] = dot_nn(x_their[...], ws_ref[...]) + bias_ref[...]
-    og_copy.wait_recv()
+    for copy in own_copies:
+        copy.wait_recv()
+    self_pre[1] = dot_nn(nodes[1, :, :BLK], ws_ref[...]) + bias_ref[...]
     links.finish(gathered)
     sides = (zh, 1 - zh)
     totals = {}
@@ -359,7 +410,10 @@
                 value = value + y_recv[p, d - 1, h].astype(F32)
             totals[k, p] = value
             zh_send[p, h] = value.astype(BF16)
-        zh_copies[p] = links.send(zh_send.at[p], zh_recv.at[p], to_zh)
+        zh_copies[p] = links.send(zh_send.at[p], zh_relay.at[p], first_leg[p])
+    for p in range(parts):
+        zh_copies[p].wait_recv()
+        zh_copies[p] = links.send(zh_relay.at[p], zh_recv.at[p], last_leg[p])
     for p in range(parts):
         zh_copies[p].wait_recv()
         for k, h in enumerate(sides):
@@ -370,7 +424,7 @@
         pre = self_pre[k] + dot_nn(sums, wn_ref[...])
         sig = 1.0 / (1.0 + jnp.exp(-pre))
         slope = sig * (1.0 + pre * (1.0 - sig))
-        return sums, pre * sig, (og_ref[k].astype(F32) * slope).astype(BF16)
+        return sums, pre * sig, (nodes[k, :, BLK:].astype(F32) * slope).astype(BF16)
 
     sums, activated, pre_grad = layer(0)
     gt[y * 2 + zh] = dot_nt(wn_ref[...], pre_grad).astype(BF16)
@@ -402,14 +456,14 @@
         copy.wait_recv()
 
     def spread(k, acc):
-        for u in range(step):
-            n = k * step + u
+        for u in range(8):
+            n = k * 8 + u
             term = dot_nn(gt[index[grow, n]], tile_buf[index[ord_c, n]])
             acc = acc * index[keep_c, n].astype(F32) + term
             runs[n] = acc
         return acc
 
-    steps = tiles // step
+    steps = tiles // 8
     acc = lax.fori_loop(0, steps // 2, spread, jnp.zeros((BLK, BLK), F32))
 
     for copy in wy_copies:
@@ -637,19 +691,20 @@
             pltpu.VMEM((feat, units), BF16),
             pltpu.VMEM((feat, units), BF16),
             pltpu.VMEM((1, units), F32),
-            pltpu.VMEM((2, BLK, units), BF16),
-            pltpu.VMEM((BLK, feat), BF16),
+            pltpu.VMEM((2, BLK, feat + units), BF16),
+            pltpu.VMEM((BLK, feat + units), BF16),
             pltpu.VMEM((1, tiles), jnp.int32),
             pltpu.VMEM((1, tiles), jnp.int32),
-            pltpu.VMEM((16, BLK), jnp.int32),
-            pltpu.SMEM((16, BLK), jnp.int32),
-            pltpu.VMEM((tiles,) + block, BF16),
+            pltpu.VMEM((8, BLK), jnp.int32),
+            pltpu.SMEM((8, BLK), jnp.int32),
+            pltpu.VMEM((tiles + 1,) + block, BF16),
             pltpu.VMEM((n_cols,) + block, BF16),
             pltpu.VMEM((tiles + 1,) + block, F32),
             pltpu.VMEM((2, BLK, units), F32),
             pltpu.VMEM(block, F32),
             halves(3, 2),
             halves(3, 2),
+            halves(2),
             halves(2),
             halves(2),
             pltpu.VMEM((n_rows,) + block, BF16),
@@ -673,7 +728,7 @@
             pltpu.VMEM((part, BLK), F32),
             pltpu.VMEM((part, BLK), F32),
             pltpu.VMEM((4,) + block, F32),
-            pltpu.SemaphoreType.DMA((9,)),
+            pltpu.SemaphoreType.DMA((10,)),
             pltpu.SemaphoreType.DMA((5,)),
             pltpu.SemaphoreType.DMA((sems,)),
             pltpu.SemaphoreType.DMA((sems,)),

time: 106 us -> 109 us (1.028)
  Pallas kernels: 105 us -> 108 us
    pallas_call x1, Pallas kernels: 103 us -> 106 us  [body(): pl.pallas_call(functools.partial(kernel, nz, tiles), out_shape=results, i...]
where the time goes in v4:
time: 109 us; the launch traced here: 108 us
  Pallas kernels  108 us (99%)
    pallas_call x1, Pallas kernels, body(): pl.pallas_call(functools.partial(kernel, nz, tiles), out_shape=results, i...  106 us

profile of v4, /device:TPU:24, one launch (start us, length us, event | category | flops | bytes accessed | tf_op | source)
XLA Modules:
  0.0 108.3 jit_solution(5920363154161782380)
XLA Ops:
  0.6 105.9 %shard_map.119 = (bf16[128,256]{1,0:T(8,128)(2,1)}, bf16[128,128]{1,0:T(8,128)(2,1)}, f32[128,256]{1,0:T(8,128)}, f32[128,256]{1,0:T(8,128)}, f32[1,256]{1,0:T(1,128)}) custom-call(bf16[128,128]{1,0:T(8,128)(2,1)} %x_hbm.1, bf16[128,256]{1,0:T(8,128)(2,1)} %ws_hbm.1, bf16[128,256]{1,0:T(8,128)(2,1)} %wn_hbm.1, f32[1,256]{1,0:T(1,128)} %bitcast.4, ...), custom_call_target="tpu_custom_call" | custom-call | flops 939524096 | bytes 3670016 | tf_op jit(solution)/shard_map/pallas_call | solution.py:684
  106.5 1.8 %shard_map.120 = (bf16[128,256]{1,0:T(8,128)(2,1)}, bf16[128,128]{1,0:T(8,128)(2,1)}, f32[128,256]{1,0:T(8,128)}, f32[128,256]{1,0:T(8,128)}, f32[1,256]{1,0:T(1,128)}) custom-call(bf16[128,256]{1,0:T(8,128)(2,1)} %get-tuple-element.15.refs_0_, bf16[128,128]{1,0:T(8,128)(2,1)} %get-tuple-element.16.refs_1_, f32[128,256]{1,0:T(8,128)} %get-tuple-element.17.refs_2_, ...), custom_call_target="tpu_custom_call" | custom-call | tf_op jit(solution)/shard_map/pallas_call | solution.py:752

commit v5 on v4

--- a/solution.py
+++ b/solution.py
@@ -137,7 +137,6 @@
     wn_ref,
     bias_ref,
     nodes,
-    nodes_relay,
     rows_ref,
     cols_ref,
     index_buf,
@@ -150,7 +149,6 @@
     y_send,
     y_recv,
     zh_send,
-    zh_relay,
     zh_recv,
     gt,
     core_send,
@@ -167,6 +165,8 @@
     wy_recv,
     wz_send,
     wz_recv,
+    wp_send,
+    wp_recv,
     wh_send,
     wh_recv,
     wx_recv,
@@ -204,9 +204,6 @@
     def lines(p):
         return pl.ds(p * width, width)
 
-    def turn_z(d):
-        return lax.rem(z + d, nz)
-
     def turn_zi(d):
         return lax.rem(zi + d, half)
 
@@ -215,9 +212,6 @@
 
     def turn_y(d):
         return lax.rem(y + d, NY)
-
-    def to_z(d):
-        return at_row(turn_z(d), x, core)
 
     def to_mate(e):
         return at_row(zq * half + turn_zi(e), x, core)
@@ -231,22 +225,14 @@
     to_pair = at_row((1 - zq) * half + zi, x, core)
     to_core = at_row(z, x, other)
     to_zh = at_col(1 - zh, y)
-
-    def along_z(d):
-        z_to = lax.rem(zh * nz + z + d, 2 * nz)
-        return {"row": (lax.rem(z_to, nz) * NX + x) * NC + core, "col": z_to // nz * NY + y}
-
-    first_leg = [along_z(nz - 1), along_z(nz + 1)]
-    last_leg = [along_z(1), along_z(2 * nz - 1)]
-    mates = [e for e in (1, half - 1) if e] + list(range(2, half - 1))
-    mates = list(dict.fromkeys(mates))
+    mates = (1, 3, 2)
 
     ord_r, pan, keep_r, end_r, ord_c, grow, keep_c, end_c = range(8)
 
-    def slot(core_of, x_of, z_of):
-        return (core_of * NX + x_of) * nz + z_of
-
-    own = slot(core, x, z)
+    def slot(core_of, x_of, e, q=0):
+        return ((core_of * NX + x_of) * half + e) * 2 + q
+
+    own = slot(core, x, 0)
     loads = []
     for src, dst in (
         (x_hbm, panels.at[own]),
@@ -264,9 +250,8 @@
     load_x, load_rows, load_cols, load_ws, load_bias, load_tiles, load_wn, load_own, load_og = loads
 
     barrier = pltpu.get_barrier_semaphore()
-    partners = [to_z(d) for d in range(1, nz)] + [to_x(d) for d in range(1, NX)]
+    partners = [to_mate(e) for e in mates] + [to_pair] + [to_x(d) for d in range(1, NX)]
     partners += [to_y(d) for d in range(1, NY)] + [to_core, to_zh]
-    partners += first_leg + last_leg
     for partner in partners:
         pl.semaphore_signal(barrier, inc=1, device_id=partner, device_id_type=MESH)
     load_x.wait()
@@ -279,97 +264,85 @@
         stores.append(pltpu.make_async_copy(src, dst, store_sems.at[len(stores)]))
         stores[-1].start()
 
-    def panel_to(slot_at, device_id):
-        return links.send(panels.at[slot_at], panels.at[slot_at], device_id)
-
-    pair_copy = panel_to(own, to_pair)
-    z_copies = {e: panel_to(own, to_mate(e)) for e in mates}
-    pair_z = (1 - zq) * half + zi
-    relayed = {}
-
-    def mate_z(e, q):
-        return q * half + turn_zi(half - e)
-
-    arrivals = [(z, None)] + [(mate_z(e, zq), z_copies[e]) for e in mates[:2]]
-    arrivals += [(pair_z, pair_copy)] + [(mate_z(e, zq), z_copies[e]) for e in mates[2:]]
-    arrivals += [(mate_z(e, 1 - zq), e) for e in mates]
-    plus, minus, far, crossed = {}, {}, {}, []
-
-    def cross(slot_at):
-        crossed.append(panel_to(slot_at, to_core))
+    def panels_to(first, count, device_id, dst=None):
+        return links.send(
+            panels.at[pl.ds(first, count)],
+            panels.at[pl.ds(first if dst is None else dst, count)],
+            device_id,
+        )
+
+    order = (0,) + mates
+    plus, minus, far, crossed, from_mate = {}, {}, {}, [], {}
+
+    def cross(x_of, i):
+        if i % 2 == 1:
+            first = slot(core, x_of, min(order[i - 1], order[i]))
+            crossed.append(panels_to(first, half, to_core))
 
     def own_step(i):
-        z_of, copy = arrivals[i]
-        here = slot(core, x, z_of)
-        if copy is not None:
-            (relayed[copy] if isinstance(copy, int) else copy).wait_recv()
-        if copy is pair_copy:
-            for e in mates:
-                relayed[e] = panel_to(here, to_mate(e))
-        plus[i] = panel_to(here, to_x(1))
-        minus[i] = panel_to(here, to_x(NX - 1))
-        cross(here)
+        e = order[i]
+        if e:
+            from_mate[e].wait_recv()
+        here = slot(core, x, e)
+        plus[i] = panels_to(here, 2, to_x(1))
+        minus[i] = panels_to(here, 2, to_x(NX - 1))
+        cross(x, i)
 
     def near_step(i):
-        z_of = arrivals[i][0]
-        from_minus = slot(core, turn_x(NX - 1), z_of)
-        from_plus = slot(core, turn_x(1), z_of)
         plus[i].wait_recv()
         if i % 2 == 0:
-            far[i] = panel_to(from_minus, to_x(1))
-        cross(from_minus)
+            far[i] = panels_to(slot(core, turn_x(NX - 1), order[i]), 2, to_x(1))
+        cross(turn_x(NX - 1), i)
         minus[i].wait_recv()
         if i % 2 == 1:
-            far[i] = panel_to(from_plus, to_x(NX - 1))
-        cross(from_plus)
+            far[i] = panels_to(slot(core, turn_x(1), order[i]), 2, to_x(NX - 1))
+        cross(turn_x(1), i)
 
     def far_step(i):
         far[i].wait_recv()
-        cross(slot(core, turn_x(2), arrivals[i][0]))
+        cross(turn_x(2), i)
+
+    index_copy = pltpu.make_async_copy(index_buf, index, load_sems.at[len(loads)])
 
     def prepare():
         load_rows.wait()
         load_cols.wait()
         rows = rows_ref[...]
         cols = cols_ref[...]
-        slots = slot(cols & (NC - 1), (cols // NC) & (NX - 1), cols // (NC * NX))
+        z_of = cols // (NC * NX)
+        e_of = (zi - z_of) & (half - 1)
+        slots = slot(cols & (NC - 1), (cols // NC) & (NX - 1), e_of, (z_of // half + zq) & 1)
         order_pairs(rows, slots, n_rows, index_buf, 0)
         order_tiles(slots, (rows & (NY - 1)) * 2 + rows // NY, n_cols, index_buf, 4)
         runs[tiles] = jnp.zeros((BLK, BLK), F32)
         tile_buf[tiles] = jnp.zeros((BLK, BLK), BF16)
-        index_copy = pltpu.make_async_copy(index_buf, index, load_sems.at[len(loads)])
         index_copy.start()
         load_ws.wait()
         load_bias.wait()
         self_pre[0] = dot_nn(panels[own], ws_ref[...]) + bias_ref[...]
-        index_copy.wait()
-
-    for i in range(nz + 2):
-        if i < nz:
+
+    pair_copy = panels_to(own, 1, to_pair, dst=own + 1)
+    prepare()
+    pair_copy.wait_recv()
+    for e in mates:
+        from_mate[e] = panels_to(own, 2, to_mate(e), dst=slot(core, x, e))
+    for i in range(half + 2):
+        if i < half:
             own_step(i)
-        if i == 0:
-            prepare()
-        if i == nz - 1:
+        if i == half - 1:
             load_own.wait()
             load_og.wait()
-            own_copies = [
-                links.send(nodes.at[0, lines(p)], nodes_relay.at[lines(p)], first_leg[p])
-                for p in range(parts)
-            ]
-        if 0 <= i - 1 < nz:
+            own_copy = links.send(nodes.at[0], nodes.at[1], to_zh)
+        if 0 <= i - 1 < half:
             near_step(i - 1)
-        if 0 <= i - 2 < nz:
+        if 0 <= i - 2 < half:
             far_step(i - 2)
     load_tiles.wait()
     load_wn.wait()
+    index_copy.wait()
     for copy in crossed:
         copy.wait_recv()
     gathered = len(links.copies)
-    for p in range(parts):
-        own_copies[p].wait_recv()
-        own_copies[p] = links.send(
-            nodes_relay.at[lines(p)], nodes.at[1, lines(p)], last_leg[p]
-        )
 
     n_pairs = (tiles + n_rows) // 2
     step = 4
@@ -386,41 +359,35 @@
 
     lax.fori_loop(0, n_pairs // step, collect, jnp.zeros((BLK, BLK), F32))
 
-    def row_sum(r, p):
-        return runs[index[end_r, r], lines(p), :]
-
-    y_copies, zh_copies = {}, {}
-    for p in range(parts):
-        for d in (2, 1, 3):
-            for h in range(2):
-                y_send[p, d - 1, h] = row_sum(h * NY + turn_y(d), p).astype(BF16)
-            y_copies[p, d] = links.send(y_send.at[p, d - 1], y_recv.at[p, d - 1], to_y(d))
-    for copy in own_copies:
-        copy.wait_recv()
+    def row_sum(r):
+        return runs[index[end_r, r]]
+
+    y_copies = {}
+    for d in (2, 1, 3):
+        for h in range(2):
+            y_send[d - 1, h] = row_sum(h * NY + turn_y(d)).astype(BF16)
+        y_copies[d] = links.send(y_send.at[d - 1], y_recv.at[d - 1], to_y(d))
+    own_copy.wait_recv()
     self_pre[1] = dot_nn(nodes[1, :, :BLK], ws_ref[...]) + bias_ref[...]
     links.finish(gathered)
     sides = (zh, 1 - zh)
-    totals = {}
-    for p in range(parts):
+    for d in (1, 3, 2):
+        y_copies[d].wait_recv()
+    totals = []
+    for h in sides:
+        value = row_sum(h * NY + y)
         for d in (1, 3, 2):
-            y_copies[p, d].wait_recv()
-        for k, h in enumerate(sides):
-            value = row_sum(h * NY + y, p)
-            for d in (1, 3, 2):
-                value = value + y_recv[p, d - 1, h].astype(F32)
-            totals[k, p] = value
-            zh_send[p, h] = value.astype(BF16)
-        zh_copies[p] = links.send(zh_send.at[p], zh_relay.at[p], first_leg[p])
-    for p in range(parts):
-        zh_copies[p].wait_recv()
-        zh_copies[p] = links.send(zh_relay.at[p], zh_recv.at[p], last_leg[p])
-    for p in range(parts):
-        zh_copies[p].wait_recv()
-        for k, h in enumerate(sides):
-            totals[k, p] = (totals[k, p] + zh_recv[p, h].astype(F32)).astype(BF16)
+            value = value + y_recv[d - 1, h].astype(F32)
+        totals.append(value)
+        zh_send[h] = value.astype(BF16)
+    zh_copy = links.send(zh_send, zh_recv, to_zh)
+    zh_copy.wait_recv()
+    totals = [
+        (value + zh_recv[h].astype(F32)).astype(BF16) for value, h in zip(totals, sides)
+    ]
 
     def layer(k):
-        sums = jnp.concatenate([totals[k, p] for p in range(parts)], axis=0)
+        sums = totals[k]
         pre = self_pre[k] + dot_nn(sums, wn_ref[...])
         sig = 1.0 / (1.0 + jnp.exp(-pre))
         slope = sig * (1.0 + pre * (1.0 - sig))
@@ -471,60 +438,54 @@
     w_sum = wy_recv[0].astype(F32)
     for q in range(1, NY):
         w_sum = w_sum + wy_recv[q].astype(F32)
-    part = BLK // nz
-    for q in range(nz):
+    part = BLK // half
+    for q in range(half):
         wz_send[q, :part] = w_sum[q * part : (q + 1) * part]
         wz_send[q, part:] = w_sum[BLK : BLK + 8]
-    wz_recv[z] = wz_send[z]
-    wz_copies = [links.send(wz_send.at[turn_z(d)], wz_recv.at[z], to_z(d)) for d in range(1, nz)]
+    wz_recv[zi] = wz_send[zi]
+    wz_copies = [links.send(wz_send.at[turn_zi(e)], wz_recv.at[zi], to_mate(e)) for e in mates]
 
     lax.fori_loop(steps // 2, steps, spread, acc)
 
-    def chunk(core_of, d):
-        return slot(core_of, turn_x(d), 0)
+    turns = (2, 1, 3, 0)
 
     def col_sum(c, p):
         return runs[index[end_c, c], lines(p), :]
 
     def paired(p, d, i):
-        return col_sum(chunk(core, d) + i, p) + core_recv[p, turn_x(d) * nz + i].astype(F32)
+        mine = col_sum(slot(core, turn_x(d), 0) + i, p)
+        return mine + core_recv[p, turns.index(d) * nz + i].astype(F32)
 
     lower, upper = pl.ds(0, half), pl.ds(half, half)
     core_copies, far_copies, near_copies, quad_copies, pair_copies = {}, {}, {}, {}, {}
 
     def core_stage(p):
-        for d in (2, 1, 3, 0):
-            base, first = chunk(other, d), turn_x(d) * nz
+        for at, d in enumerate(turns):
             for i in range(nz):
-                core_send[p, first + i] = col_sum(base + i, p).astype(BF16)
-            blocks = pl.ds(first, nz)
-            core_copies[p, d] = links.send(
-                core_send.at[p, blocks], core_recv.at[p, blocks], to_core
-            )
+                core_send[p, at * nz + i] = col_sum(slot(other, turn_x(d), 0) + i, p).astype(BF16)
+            if at in (0, NX - 1):
+                blocks = pl.ds(0, nz) if at == 0 else pl.ds(nz, (NX - 1) * nz)
+                core_copies[p, at] = links.send(
+                    core_send.at[p, blocks], core_recv.at[p, blocks], to_core
+                )
 
     def far_stage(p):
-        core_copies[p, 2].wait_recv()
+        core_copies[p, 0].wait_recv()
         for i in range(nz):
             far_send[p, i] = paired(p, 2, i).astype(BF16)
         far_copies[p, 0] = links.send(far_send.at[p, lower], far_recv.at[p, lower], to_x(1))
         far_copies[p, 1] = links.send(far_send.at[p, upper], far_recv.at[p, upper], to_x(NX - 1))
 
-    def near_stage(p, way, with_far):
-        d = (1, NX - 1)[way]
-        if with_far:
+    def near_stage(p):
+        core_copies[p, NX - 1].wait_recv()
+        for way, d in enumerate((1, NX - 1)):
             far_copies[p, way].wait_recv()
-        else:
-            core_copies[p, d].wait_recv()
-        first = half * (way if with_far else 1 - way)
-        for i in range(first, first + half):
-            value = paired(p, d, i)
-            if with_far:
-                value = value + far_recv[p, i].astype(F32)
-            near_send[p, way, i] = value.astype(BF16)
-        blocks = pl.ds(first, half)
-        near_copies[p, way, with_far] = links.send(
-            near_send.at[p, way, blocks], near_recv.at[p, way, blocks], to_x(d)
-        )
+            for i in range(nz):
+                value = paired(p, d, i)
+                if i // half == way:
+                    value = value + far_recv[p, i].astype(F32)
+                near_send[p, way, i] = value.astype(BF16)
+            near_copies[p, way] = links.send(near_send.at[p, way], near_recv.at[p, way], to_x(d))
 
     def z_total(p, i):
         return (
@@ -532,17 +493,17 @@
         )
 
     def quad_stage(p):
-        core_copies[p, 0].wait_recv()
         for way in range(2):
-            for with_far in (False, True):
-                near_copies[p, way, with_far].wait_recv()
+            near_copies[p, way].wait_recv()
         for e in mates:
-            quad_send[p, e, 0] = z_total(p, zq * half + turn_zi(e)).astype(BF16)
-            quad_send[p, e, 1] = z_total(p, (1 - zq) * half + turn_zi(e)).astype(BF16)
-            quad_copies[p, e] = links.send(quad_send.at[p, e], quad_recv.at[p, e], to_mate(e))
+            for q in range(2):
+                quad_send[p, e, q] = z_total(p, 2 * e + q).astype(BF16)
+            quad_copies[p, e] = links.send(
+                quad_send.at[p, e], quad_recv.at[p, e], to_mate(half - e)
+            )
 
     def pair_stage(p):
-        value = z_total(p, pair_z)
+        value = z_total(p, 1)
         for e in mates:
             quad_copies[p, e].wait_recv()
             value = value + quad_recv[p, e, 1].astype(F32)
@@ -550,39 +511,38 @@
         pair_copies[p] = links.send(pair_send.at[p], pair_recv.at[p], to_pair)
 
     def last_stage(p):
-        value = z_total(p, z) + self_grad[lines(p), :]
+        value = z_total(p, 0) + self_grad[lines(p), :]
         for e in mates:
             value = value + quad_recv[p, e, 0].astype(F32)
         pair_copies[p].wait_recv()
         return value + pair_recv[p].astype(F32)
 
-    for p in range(parts):
-        core_stage(p)
-    far_stage(0)
-    near_stage(0, 0, False)
-    near_stage(0, 1, False)
-
     for copy in wz_copies:
         copy.wait_recv()
     w_part = wz_recv[0]
-    for q in range(1, nz):
+    for q in range(1, half):
         w_part = w_part + wz_recv[q]
+    wp_send[...] = w_part
+    wp_copy = links.send(wp_send, wp_recv, to_pair)
+
+    core_stage(0)
+    core_stage(1)
+
+    wp_copy.wait_recv()
+    w_part = w_part + wp_recv[...]
     wh_send[...] = w_part
     wh_copy = links.send(wh_send, wh_recv, to_zh)
 
+    far_stage(0)
     far_stage(1)
-    near_stage(0, 0, True)
-    near_stage(0, 1, True)
-    near_stage(1, 0, False)
-    near_stage(1, 1, False)
+    near_stage(0)
 
     wh_copy.wait_recv()
     w_part = w_part + wh_recv[...]
     wx_recv[x] = w_part
     wx_copies = [links.send(wx_recv.at[x], wx_recv.at[x], to_x(d)) for d in (2, 1, 3)]
 
-    near_stage(1, 0, True)
-    near_stage(1, 1, True)
+    near_stage(1)
     quad_stage(0)
 
     for copy in wx_copies:
@@ -594,7 +554,6 @@
     wc_copy = links.send(wc_send, wc_recv, to_core)
 
     pair_stage(0)
-    quad_stage(1)
 
     wc_copy.wait_recv()
     w_part = w_part + wc_recv[...]
@@ -602,17 +561,18 @@
         [w_part[part : part + 1], w_part[part + 1 : part + 2]], axis=1
     )
     store(gbias_ref, gbias_hbm)
-    rows_here = pl.ds(pl.multiple_of(z * part, part), part)
+    rows_here = pl.ds(pl.multiple_of(zi * part, part), part)
     w_out[y, rows_here] = w_part[:part]
     gz_copies = [
-        links.send(w_out.at[y, rows_here], w_out.at[y, rows_here], to_z(d)) for d in range(1, nz)
+        links.send(w_out.at[y, rows_here], w_out.at[y, rows_here], to_mate(e)) for e in mates
     ]
 
-    pair_stage(1)
-    links.finish(len(links.copies) - nz)
+    quad_stage(1)
     for copy in gz_copies:
         copy.wait_recv()
     gy_copies = [links.send(w_out.at[y], w_out.at[y], to_y(d)) for d in (2, 1, 3)]
+    pair_stage(1)
+    links.finish(len(links.copies) - 8)
     grad = jnp.concatenate([last_stage(p) for p in range(parts)], axis=0)
     ingrad_ref[...] = jnp.transpose(grad).astype(BF16)
     store(ingrad_ref, ingrad_hbm)
@@ -668,7 +628,7 @@
     hbm = pl.BlockSpec(memory_space=pltpu.HBM)
     block = (BLK, BLK)
     lines = (2, BLK // 2, BLK)
-    part = BLK // nz + 8
+    part = BLK // half + 8
     sems = 256
     results = (
         jax.ShapeDtypeStruct((BLK, units), BF16),
@@ -692,7 +652,6 @@
             pltpu.VMEM((feat, units), BF16),
             pltpu.VMEM((1, units), F32),
             pltpu.VMEM((2, BLK, feat + units), BF16),
-            pltpu.VMEM((BLK, feat + units), BF16),
             pltpu.VMEM((1, tiles), jnp.int32),
             pltpu.VMEM((1, tiles), jnp.int32),
             pltpu.VMEM((8, BLK), jnp.int32),
@@ -702,11 +661,10 @@
             pltpu.VMEM((tiles + 1,) + block, F32),
             pltpu.VMEM((2, BLK, units), F32),
             pltpu.VMEM(block, F32),
-            halves(3, 2),
-            halves(3, 2),
-            halves(2),
-            halves(2),
-            halves(2),
+            pltpu.VMEM((3, 2) + block, BF16),
+            pltpu.VMEM((3, 2) + block, BF16),
+            pltpu.VMEM((2,) + block, BF16),
+            pltpu.VMEM((2,) + block, BF16),
             pltpu.VMEM((n_rows,) + block, BF16),
             halves(NX * nz),
             halves(NX * nz),
@@ -720,8 +678,10 @@
             halves(),
             pltpu.VMEM((4, BLK + 16, BLK), BF16),
             pltpu.VMEM((4, BLK + 16, BLK), BF16),
-            pltpu.VMEM((nz, part, BLK), F32),
-            pltpu.VMEM((nz, part, BLK), F32),
+            pltpu.VMEM((half, part, BLK), F32),
+            pltpu.VMEM((half, part, BLK), F32),
+            pltpu.VMEM((part, BLK), F32),
+            pltpu.VMEM((part, BLK), F32),
             pltpu.VMEM((part, BLK), F32),
             pltpu.VMEM((part, BLK), F32),
             pltpu.VMEM((NX, part, BLK), F32),

time: 109 us -> 107 us (0.982)
  Pallas kernels: 108 us -> 105 us
    pallas_call x1, Pallas kernels: 106 us -> 103 us  [body(): pl.pallas_call(functools.partial(kernel, nz, tiles), out_shape=results, i...]
where the time goes in v5:
time: 107 us; the launch traced here: 105 us
  Pallas kernels  105 us (98%)
    pallas_call x1, Pallas kernels, body(): pl.pallas_call(functools.partial(kernel, nz, tiles), out_shape=results, i...  103 us

profile of v5, /device:TPU:24, one launch (start us, length us, event | category | flops | bytes accessed | tf_op | source)
XLA Modules:
  0.0 105.3 jit_solution(4402692985969562799)
XLA Ops:
  0.6 102.9 %shard_map.119 = (bf16[128,256]{1,0:T(8,128)(2,1)}, bf16[128,128]{1,0:T(8,128)(2,1)}, f32[128,256]{1,0:T(8,128)}, f32[128,256]{1,0:T(8,128)}, f32[1,256]{1,0:T(1,128)}) custom-call(bf16[128,128]{1,0:T(8,128)(2,1)} %x_hbm.1, bf16[128,256]{1,0:T(8,128)(2,1)} %ws_hbm.1, bf16[128,256]{1,0:T(8,128)(2,1)} %wn_hbm.1, f32[1,256]{1,0:T(1,128)} %bitcast.4, ...), custom_call_target="tpu_custom_call" | custom-call | flops 939524096 | bytes 3670016 | tf_op jit(solution)/shard_map/pallas_call | solution.py:644
  103.5 1.8 %shard_map.120 = (bf16[128,256]{1,0:T(8,128)(2,1)}, bf16[128,128]{1,0:T(8,128)(2,1)}, f32[128,256]{1,0:T(8,128)}, f32[128,256]{1,0:T(8,128)}, f32[1,256]{1,0:T(1,128)}) custom-call(bf16[128,256]{1,0:T(8,128)(2,1)} %get-tuple-element.15.refs_0_, bf16[128,128]{1,0:T(8,128)(2,1)} %get-tuple-element.16.refs_1_, f32[128,256]{1,0:T(8,128)} %get-tuple-element.17.refs_2_, ...), custom_call_target="tpu_custom_call" | custom-call | tf_op jit(solution)/shard_map/pallas_call | solution.py:712

commit v6 on v5

--- a/solution.py
+++ b/solution.py
@@ -12,6 +12,7 @@
 F32 = jnp.float32
 BF16 = jnp.bfloat16
 VMEM_LIMIT = 64 * 2**20
+PARTS = 4
 
 NX, NC = 4, 2
 NY = 4
@@ -198,7 +199,7 @@
     def at_col(zh_to, y_to):
         return {"row": row, "col": zh_to * NY + y_to}
 
-    parts = 2
+    parts = PARTS
     width = BLK // parts
 
     def lines(p):
@@ -230,7 +231,7 @@
     ord_r, pan, keep_r, end_r, ord_c, grow, keep_c, end_c = range(8)
 
     def slot(core_of, x_of, e, q=0):
-        return ((core_of * NX + x_of) * half + e) * 2 + q
+        return ((core_of * NX + x_of) * 2 + q) * half + e
 
     own = slot(core, x, 0)
     loads = []
@@ -271,31 +272,36 @@
             device_id,
         )
 
-    order = (0,) + mates
-    plus, minus, far, crossed, from_mate = {}, {}, {}, [], {}
+    order = [(0, 0), (1, 0), (3, 0), (0, 1), (2, 0), (1, 1), (3, 1), (2, 1)]
+    along = {(0, 1): panels_to(own, 1, to_pair, dst=slot(core, x, 0, 1))}
+    for e in mates:
+        along[e, 0] = panels_to(own, 1, to_mate(e), dst=slot(core, x, e))
+    plus, minus, far, crossed = {}, {}, {}, []
 
     def cross(x_of, i):
-        if i % 2 == 1:
-            first = slot(core, x_of, min(order[i - 1], order[i]))
-            crossed.append(panels_to(first, half, to_core))
+        if i in (half, nz - 1):
+            crossed.append(panels_to(slot(core, x_of, 0, order[i][1]), half, to_core))
 
     def own_step(i):
-        e = order[i]
-        if e:
-            from_mate[e].wait_recv()
-        here = slot(core, x, e)
-        plus[i] = panels_to(here, 2, to_x(1))
-        minus[i] = panels_to(here, 2, to_x(NX - 1))
+        e, q = order[i]
+        here = slot(core, x, e, q)
+        if i:
+            along[e, q].wait_recv()
+        if (e, q) == (0, 1):
+            for m in mates:
+                along[m, 1] = panels_to(here, 1, to_mate(m), dst=slot(core, x, m, 1))
+        plus[i] = panels_to(here, 1, to_x(1))
+        minus[i] = panels_to(here, 1, to_x(NX - 1))
         cross(x, i)
 
     def near_step(i):
         plus[i].wait_recv()
         if i % 2 == 0:
-            far[i] = panels_to(slot(core, turn_x(NX - 1), order[i]), 2, to_x(1))
+            far[i] = panels_to(slot(core, turn_x(NX - 1), *order[i]), 1, to_x(1))
         cross(turn_x(NX - 1), i)
         minus[i].wait_recv()
         if i % 2 == 1:
-            far[i] = panels_to(slot(core, turn_x(1), order[i]), 2, to_x(NX - 1))
+            far[i] = panels_to(slot(core, turn_x(1), *order[i]), 1, to_x(NX - 1))
         cross(turn_x(1), i)
 
     def far_step(i):
@@ -321,21 +327,18 @@
         load_bias.wait()
         self_pre[0] = dot_nn(panels[own], ws_ref[...]) + bias_ref[...]
 
-    pair_copy = panels_to(own, 1, to_pair, dst=own + 1)
-    prepare()
-    pair_copy.wait_recv()
-    for e in mates:
-        from_mate[e] = panels_to(own, 2, to_mate(e), dst=slot(core, x, e))
-    for i in range(half + 2):
-        if i < half:
+    for i in range(nz + 2):
+        if i < nz:
             own_step(i)
-        if i == half - 1:
+        if i == 0:
+            prepare()
+        if i == nz - 1:
             load_own.wait()
             load_og.wait()
             own_copy = links.send(nodes.at[0], nodes.at[1], to_zh)
-        if 0 <= i - 1 < half:
+        if 0 <= i - 1 < nz:
             near_step(i - 1)
-        if 0 <= i - 2 < half:
+        if 0 <= i - 2 < nz:
             far_step(i - 2)
     load_tiles.wait()
     load_wn.wait()
@@ -359,35 +362,39 @@
 
     lax.fori_loop(0, n_pairs // step, collect, jnp.zeros((BLK, BLK), F32))
 
-    def row_sum(r):
-        return runs[index[end_r, r]]
-
-    y_copies = {}
-    for d in (2, 1, 3):
-        for h in range(2):
-            y_send[d - 1, h] = row_sum(h * NY + turn_y(d)).astype(BF16)
-        y_copies[d] = links.send(y_send.at[d - 1], y_recv.at[d - 1], to_y(d))
+    def piece(p):
+        return pl.ds(p * (BLK // 2), BLK // 2)
+
+    def row_sum(r, p):
+        return runs[index[end_r, r], piece(p), :]
+
+    y_copies, zh_copies, totals = {}, {}, {}
+    for p in range(2):
+        for d in (2, 1, 3):
+            for h in range(2):
+                y_send[p, d - 1, h] = row_sum(h * NY + turn_y(d), p).astype(BF16)
+            y_copies[p, d] = links.send(y_send.at[p, d - 1], y_recv.at[p, d - 1], to_y(d))
     own_copy.wait_recv()
     self_pre[1] = dot_nn(nodes[1, :, :BLK], ws_ref[...]) + bias_ref[...]
     links.finish(gathered)
     sides = (zh, 1 - zh)
-    for d in (1, 3, 2):
-        y_copies[d].wait_recv()
-    totals = []
-    for h in sides:
-        value = row_sum(h * NY + y)
+    for p in range(2):
         for d in (1, 3, 2):
-            value = value + y_recv[d - 1, h].astype(F32)
-        totals.append(value)
-        zh_send[h] = value.astype(BF16)
-    zh_copy = links.send(zh_send, zh_recv, to_zh)
-    zh_copy.wait_recv()
-    totals = [
-        (value + zh_recv[h].astype(F32)).astype(BF16) for value, h in zip(totals, sides)
-    ]
+            y_copies[p, d].wait_recv()
+        for k, h in enumerate(sides):
+            value = row_sum(h * NY + y, p)
+            for d in (1, 3, 2):
+                value = value + y_recv[p, d - 1, h].astype(F32)
+            totals[k, p] = value
+            zh_send[p, h] = value.astype(BF16)
+        zh_copies[p] = links.send(zh_send.at[p], zh_recv.at[p], to_zh)
+    for p in range(2):
+        zh_copies[p].wait_recv()
+        for k, h in enumerate(sides):
+            totals[k, p] = (totals[k, p] + zh_recv[p, h].astype(F32)).astype(BF16)
 
     def layer(k):
-        sums = totals[k]
+        sums = jnp.concatenate([totals[k, 0], totals[k, 1]], axis=0)
         pre = self_pre[k] + dot_nn(sums, wn_ref[...])
         sig = 1.0 / (1.0 + jnp.exp(-pre))
         slope = sig * (1.0 + pre * (1.0 - sig))
@@ -497,13 +504,13 @@
             near_copies[p, way].wait_recv()
         for e in mates:
             for q in range(2):
-                quad_send[p, e, q] = z_total(p, 2 * e + q).astype(BF16)
+                quad_send[p, e, q] = z_total(p, q * half + e).astype(BF16)
             quad_copies[p, e] = links.send(
                 quad_send.at[p, e], quad_recv.at[p, e], to_mate(half - e)
             )
 
     def pair_stage(p):
-        value = z_total(p, 1)
+        value = z_total(p, half)
         for e in mates:
             quad_copies[p, e].wait_recv()
             value = value + quad_recv[p, e, 1].astype(F32)
@@ -534,8 +541,11 @@
     wh_copy = links.send(wh_send, wh_recv, to_zh)
 
     far_stage(0)
+    core_stage(2)
     far_stage(1)
     near_stage(0)
+    core_stage(3)
+    far_stage(2)
 
     wh_copy.wait_recv()
     w_part = w_part + wh_recv[...]
@@ -544,6 +554,10 @@
 
     near_stage(1)
     quad_stage(0)
+    far_stage(3)
+    near_stage(2)
+    quad_stage(1)
+    pair_stage(0)
 
     for copy in wx_copies:
         copy.wait_recv()
@@ -553,7 +567,9 @@
     wc_send[...] = w_part
     wc_copy = links.send(wc_send, wc_recv, to_core)
 
-    pair_stage(0)
+    near_stage(3)
+    quad_stage(2)
+    pair_stage(1)
 
     wc_copy.wait_recv()
     w_part = w_part + wc_recv[...]
@@ -562,16 +578,17 @@
     )
     store(gbias_ref, gbias_hbm)
     rows_here = pl.ds(pl.multiple_of(zi * part, part), part)
-    w_out[y, rows_here] = w_part[:part]
+    w_out[y, rows_here] = w_part[:part].astype(BF16)
     gz_copies = [
         links.send(w_out.at[y, rows_here], w_out.at[y, rows_here], to_mate(e)) for e in mates
     ]
 
-    quad_stage(1)
+    quad_stage(3)
+    pair_stage(2)
     for copy in gz_copies:
         copy.wait_recv()
     gy_copies = [links.send(w_out.at[y], w_out.at[y], to_y(d)) for d in (2, 1, 3)]
-    pair_stage(1)
+    pair_stage(3)
     links.finish(len(links.copies) - 8)
     grad = jnp.concatenate([last_stage(p) for p in range(parts)], axis=0)
     ingrad_ref[...] = jnp.transpose(grad).astype(BF16)
@@ -579,10 +596,10 @@
 
     for copy in gy_copies:
         copy.wait_recv()
-    gself_ref[:, :BLK] = w_out[0]
-    gself_ref[:, BLK:] = w_out[1]
-    gneigh_ref[:, :BLK] = w_out[2]
-    gneigh_ref[:, BLK:] = w_out[3]
+    gself_ref[:, :BLK] = w_out[0].astype(F32)
+    gself_ref[:, BLK:] = w_out[1].astype(F32)
+    gneigh_ref[:, :BLK] = w_out[2].astype(F32)
+    gneigh_ref[:, BLK:] = w_out[3].astype(F32)
     store(gself_ref, gself_hbm)
     store(gneigh_ref, gneigh_hbm)
     links.finish()
@@ -638,8 +655,8 @@
         jax.ShapeDtypeStruct((1, units), F32),
     )
 
-    def halves(*lead):
-        return pltpu.VMEM((2,) + lead + (BLK // 2, BLK), BF16)
+    def pieces(*lead):
+        return pltpu.VMEM((PARTS,) + lead + (BLK // PARTS, BLK), BF16)
 
     outs = pl.pallas_call(
         functools.partial(kernel, nz, tiles),
@@ -661,21 +678,21 @@
             pltpu.VMEM((tiles + 1,) + block, F32),
             pltpu.VMEM((2, BLK, units), F32),
             pltpu.VMEM(block, F32),
-            pltpu.VMEM((3, 2) + block, BF16),
-            pltpu.VMEM((3, 2) + block, BF16),
-            pltpu.VMEM((2,) + block, BF16),
-            pltpu.VMEM((2,) + block, BF16),
+            pltpu.VMEM((2, 3, 2, BLK // 2, BLK), BF16),
+            pltpu.VMEM((2, 3, 2, BLK // 2, BLK), BF16),
+            pltpu.VMEM((2, 2, BLK // 2, BLK), BF16),
+            pltpu.VMEM((2, 2, BLK // 2, BLK), BF16),
             pltpu.VMEM((n_rows,) + block, BF16),
-            halves(NX * nz),
-            halves(NX * nz),
-            halves(nz),
-            halves(nz),
-            halves(2, nz),
-            halves(2, nz),
-            halves(half, 2),
-            halves(half, 2),
-            halves(),
-            halves(),
+            pieces(NX * nz),
+            pieces(NX * nz),
+            pieces(nz),
+            pieces(nz),
+            pieces(2, nz),
+            pieces(2, nz),
+            pieces(half, 2),
+            pieces(half, 2),
+            pieces(),
+            pieces(),
             pltpu.VMEM((4, BLK + 16, BLK), BF16),
             pltpu.VMEM((4, BLK + 16, BLK), BF16),
             pltpu.VMEM((half, part, BLK), F32),
@@ -687,7 +704,7 @@
             pltpu.VMEM((NX, part, BLK), F32),
             pltpu.VMEM((part, BLK), F32),
             pltpu.VMEM((part, BLK), F32),
-            pltpu.VMEM((4,) + block, F32),
+            pltpu.VMEM((4,) + block, BF16),
             pltpu.SemaphoreType.DMA((10,)),
             pltpu.SemaphoreType.DMA((5,)),
             pltpu.SemaphoreType.DMA((sems,)),

time: 107 us -> 110 us (1.028); the launches traced: 105 us -> 110 us
  Pallas kernels: 105 us -> 109 us
    pallas_call x1, Pallas kernels: 103 us -> 108 us  [body(): pl.pallas_call(functools.partial(kernel, nz, tiles), out_shape=results, i...]
where the time goes in v6:
time: 110 us
  Pallas kernels  109 us (99%)
    pallas_call x1, Pallas kernels, body(): pl.pallas_call(functools.partial(kernel, nz, tiles), out_shape=results, i...  108 us

profile of v6, /device:TPU:24, one launch (start us, length us, event | category | flops | bytes accessed | tf_op | source)
XLA Modules:
  0.0 110.0 jit_solution(6037258738800003521)
XLA Ops:
  0.6 107.6 %shard_map.119 = (bf16[128,256]{1,0:T(8,128)(2,1)}, bf16[128,128]{1,0:T(8,128)(2,1)}, f32[128,256]{1,0:T(8,128)}, f32[128,256]{1,0:T(8,128)}, f32[1,256]{1,0:T(1,128)}) custom-call(bf16[128,128]{1,0:T(8,128)(2,1)} %x_hbm.1, bf16[128,256]{1,0:T(8,128)(2,1)} %ws_hbm.1, bf16[128,256]{1,0:T(8,128)(2,1)} %wn_hbm.1, f32[1,256]{1,0:T(1,128)} %bitcast.4, ...), custom_call_target="tpu_custom_call" | custom-call | flops 939524096 | bytes 3670016 | tf_op jit(solution)/shard_map/pallas_call | solution.py:661
  108.2 1.8 %shard_map.120 = (bf16[128,256]{1,0:T(8,128)(2,1)}, bf16[128,128]{1,0:T(8,128)(2,1)}, f32[128,256]{1,0:T(8,128)}, f32[128,256]{1,0:T(8,128)}, f32[1,256]{1,0:T(1,128)}) custom-call(bf16[128,256]{1,0:T(8,128)(2,1)} %get-tuple-element.15.refs_0_, bf16[128,128]{1,0:T(8,128)(2,1)} %get-tuple-element.16.refs_1_, f32[128,256]{1,0:T(8,128)} %get-tuple-element.17.refs_2_, ...), custom_call_target="tpu_custom_call" | custom-call | tf_op jit(solution)/shard_map/pallas_call | solution.py:729

commit v7 on v5

--- a/solution.py
+++ b/solution.py
@@ -153,10 +153,8 @@
     gt,
     core_send,
     core_recv,
-    far_send,
-    far_recv,
-    near_send,
-    near_recv,
+    x_send,
+    x_recv,
     quad_send,
     quad_recv,
     pair_send,
@@ -272,7 +270,8 @@
         )
 
     order = (0,) + mates
-    plus, minus, far, crossed, from_mate = {}, {}, {}, [], {}
+    steps_x = (2, 1, 3)
+    along_x, crossed, from_mate = {}, [], {}
 
     def cross(x_of, i):
         if i % 2 == 1:
@@ -284,23 +283,14 @@
         if e:
             from_mate[e].wait_recv()
         here = slot(core, x, e)
-        plus[i] = panels_to(here, 2, to_x(1))
-        minus[i] = panels_to(here, 2, to_x(NX - 1))
+        for d in steps_x:
+            along_x[i, d] = panels_to(here, 2, to_x(d))
         cross(x, i)
 
-    def near_step(i):
-        plus[i].wait_recv()
-        if i % 2 == 0:
-            far[i] = panels_to(slot(core, turn_x(NX - 1), order[i]), 2, to_x(1))
-        cross(turn_x(NX - 1), i)
-        minus[i].wait_recv()
-        if i % 2 == 1:
-            far[i] = panels_to(slot(core, turn_x(1), order[i]), 2, to_x(NX - 1))
-        cross(turn_x(1), i)
-
-    def far_step(i):
-        far[i].wait_recv()
-        cross(turn_x(2), i)
+    def near_step(i, distances):
+        for d in distances:
+            along_x[i, d].wait_recv()
+            cross(turn_x(NX - d), i)
 
     index_copy = pltpu.make_async_copy(index_buf, index, load_sems.at[len(loads)])
 
@@ -322,21 +312,22 @@
         self_pre[0] = dot_nn(panels[own], ws_ref[...]) + bias_ref[...]
 
     pair_copy = panels_to(own, 1, to_pair, dst=own + 1)
-    prepare()
     pair_copy.wait_recv()
     for e in mates:
         from_mate[e] = panels_to(own, 2, to_mate(e), dst=slot(core, x, e))
     for i in range(half + 2):
         if i < half:
             own_step(i)
+        if i == 0:
+            prepare()
         if i == half - 1:
             load_own.wait()
             load_og.wait()
             own_copy = links.send(nodes.at[0], nodes.at[1], to_zh)
         if 0 <= i - 1 < half:
-            near_step(i - 1)
+            near_step(i - 1, (1, 3))
         if 0 <= i - 2 < half:
-            far_step(i - 2)
+            near_step(i - 2, (2,))
     load_tiles.wait()
     load_wn.wait()
     index_copy.wait()
@@ -456,8 +447,7 @@
         mine = col_sum(slot(core, turn_x(d), 0) + i, p)
         return mine + core_recv[p, turns.index(d) * nz + i].astype(F32)
 
-    lower, upper = pl.ds(0, half), pl.ds(half, half)
-    core_copies, far_copies, near_copies, quad_copies, pair_copies = {}, {}, {}, {}, {}
+    core_copies, x_copies, quad_copies, pair_copies = {}, {}, {}, {}
 
     def core_stage(p):
         for at, d in enumerate(turns):
@@ -469,32 +459,23 @@
                     core_send.at[p, blocks], core_recv.at[p, blocks], to_core
                 )
 
-    def far_stage(p):
-        core_copies[p, 0].wait_recv()
-        for i in range(nz):
-            far_send[p, i] = paired(p, 2, i).astype(BF16)
-        far_copies[p, 0] = links.send(far_send.at[p, lower], far_recv.at[p, lower], to_x(1))
-        far_copies[p, 1] = links.send(far_send.at[p, upper], far_recv.at[p, upper], to_x(NX - 1))
-
-    def near_stage(p):
-        core_copies[p, NX - 1].wait_recv()
-        for way, d in enumerate((1, NX - 1)):
-            far_copies[p, way].wait_recv()
+    def x_stage(p):
+        for at, d in enumerate(steps_x):
+            if at < 2:
+                core_copies[p, at * (NX - 1)].wait_recv()
             for i in range(nz):
-                value = paired(p, d, i)
-                if i // half == way:
-                    value = value + far_recv[p, i].astype(F32)
-                near_send[p, way, i] = value.astype(BF16)
-            near_copies[p, way] = links.send(near_send.at[p, way], near_recv.at[p, way], to_x(d))
+                x_send[p, at, i] = paired(p, d, i).astype(BF16)
+            x_copies[p, d] = links.send(x_send.at[p, at], x_recv.at[p, at], to_x(d))
 
     def z_total(p, i):
-        return (
-            paired(p, 0, i) + near_recv[p, 0, i].astype(F32) + near_recv[p, 1, i].astype(F32)
-        )
+        value = paired(p, 0, i)
+        for at in range(NX - 1):
+            value = value + x_recv[p, at, i].astype(F32)
+        return value
 
     def quad_stage(p):
-        for way in range(2):
-            near_copies[p, way].wait_recv()
+        for d in steps_x:
+            x_copies[p, d].wait_recv()
         for e in mates:
             for q in range(2):
                 quad_send[p, e, q] = z_total(p, 2 * e + q).astype(BF16)
@@ -533,16 +514,14 @@
     wh_send[...] = w_part
     wh_copy = links.send(wh_send, wh_recv, to_zh)
 
-    far_stage(0)
-    far_stage(1)
-    near_stage(0)
+    x_stage(0)
 
     wh_copy.wait_recv()
     w_part = w_part + wh_recv[...]
     wx_recv[x] = w_part
     wx_copies = [links.send(wx_recv.at[x], wx_recv.at[x], to_x(d)) for d in (2, 1, 3)]
 
-    near_stage(1)
+    x_stage(1)
     quad_stage(0)
 
     for copy in wx_copies:
@@ -562,7 +541,7 @@
     )
     store(gbias_ref, gbias_hbm)
     rows_here = pl.ds(pl.multiple_of(zi * part, part), part)
-    w_out[y, rows_here] = w_part[:part]
+    w_out[y, rows_here] = w_part[:part].astype(BF16)
     gz_copies = [
         links.send(w_out.at[y, rows_here], w_out.at[y, rows_here], to_mate(e)) for e in mates
     ]
@@ -579,10 +558,10 @@
 
     for copy in gy_copies:
         copy.wait_recv()
-    gself_ref[:, :BLK] = w_out[0]
-    gself_ref[:, BLK:] = w_out[1]
-    gneigh_ref[:, :BLK] = w_out[2]
-    gneigh_ref[:, BLK:] = w_out[3]
+    gself_ref[:, :BLK] = w_out[0].astype(F32)
+    gself_ref[:, BLK:] = w_out[1].astype(F32)
+    gneigh_ref[:, :BLK] = w_out[2].astype(F32)
+    gneigh_ref[:, BLK:] = w_out[3].astype(F32)
     store(gself_ref, gself_hbm)
     store(gneigh_ref, gneigh_hbm)
     links.finish()
@@ -668,10 +647,8 @@
             pltpu.VMEM((n_rows,) + block, BF16),
             halves(NX * nz),
             halves(NX * nz),
-            halves(nz),
-            halves(nz),
-            halves(2, nz),
-            halves(2, nz),
+            halves(NX - 1, nz),
+            halves(NX - 1, nz),
             halves(half, 2),
             halves(half, 2),
             halves(),
@@ -687,7 +664,7 @@
             pltpu.VMEM((NX, part, BLK), F32),
             pltpu.VMEM((part, BLK), F32),
             pltpu.VMEM((part, BLK), F32),
-            pltpu.VMEM((4,) + block, F32),
+            pltpu.VMEM((4,) + block, BF16),
             pltpu.SemaphoreType.DMA((10,)),
             pltpu.SemaphoreType.DMA((5,)),
             pltpu.SemaphoreType.DMA((sems,)),

time: 107 us -> 104 us (0.972)
  Pallas kernels: 105 us -> 102 us
    pallas_call x1, Pallas kernels: 103 us -> 100 us  [body(): pl.pallas_call(functools.partial(kernel, nz, tiles), out_shape=results, i...]
where the time goes in v7:
time: 104 us; the launch traced here: 103 us
  Pallas kernels  102 us (98%)
    pallas_call x1, Pallas kernels, body(): pl.pallas_call(functools.partial(kernel, nz, tiles), out_shape=results, i...  100 us

profile of v7, /device:TPU:24, one launch (start us, length us, event | category | flops | bytes accessed | tf_op | source)
XLA Modules:
  0.0 102.7 jit_solution(15101094724930568418)
XLA Ops:
  0.6 100.3 %shard_map.119 = (bf16[128,256]{1,0:T(8,128)(2,1)}, bf16[128,128]{1,0:T(8,128)(2,1)}, f32[128,256]{1,0:T(8,128)}, f32[128,256]{1,0:T(8,128)}, f32[1,256]{1,0:T(1,128)}) custom-call(bf16[128,128]{1,0:T(8,128)(2,1)} %x_hbm.1, bf16[128,256]{1,0:T(8,128)(2,1)} %ws_hbm.1, bf16[128,256]{1,0:T(8,128)(2,1)} %wn_hbm.1, f32[1,256]{1,0:T(1,128)} %bitcast.4, ...), custom_call_target="tpu_custom_call" | custom-call | flops 939524096 | bytes 3670016 | tf_op jit(solution)/shard_map/pallas_call | solution.py:623
  101.0 1.8 %shard_map.120 = (bf16[128,256]{1,0:T(8,128)(2,1)}, bf16[128,128]{1,0:T(8,128)(2,1)}, f32[128,256]{1,0:T(8,128)}, f32[128,256]{1,0:T(8,128)}, f32[1,256]{1,0:T(1,128)}) custom-call(bf16[128,256]{1,0:T(8,128)(2,1)} %get-tuple-element.15.refs_0_, bf16[128,128]{1,0:T(8,128)(2,1)} %get-tuple-element.16.refs_1_, f32[128,256]{1,0:T(8,128)} %get-tuple-element.17.refs_2_, ...), custom_call_target="tpu_custom_call" | custom-call | tf_op jit(solution)/shard_map/pallas_call | solution.py:689

commit v8 on v7

--- a/solution.py
+++ b/solution.py
@@ -155,10 +155,8 @@
     core_recv,
     x_send,
     x_recv,
-    quad_send,
-    quad_recv,
-    pair_send,
-    pair_recv,
+    z_send,
+    z_recv,
     wy_send,
     wy_recv,
     wz_send,
@@ -220,6 +218,9 @@
     def to_y(d):
         return at_col(zh, turn_y(d))
 
+    def to_far(e):
+        return at_row((1 - zq) * half + turn_zi(e), x, core)
+
     to_pair = at_row((1 - zq) * half + zi, x, core)
     to_core = at_row(z, x, other)
     to_zh = at_col(1 - zh, y)
@@ -248,7 +249,7 @@
     load_x, load_rows, load_cols, load_ws, load_bias, load_tiles, load_wn, load_own, load_og = loads
 
     barrier = pltpu.get_barrier_semaphore()
-    partners = [to_mate(e) for e in mates] + [to_pair] + [to_x(d) for d in range(1, NX)]
+    partners = [to_mate(e) for e in mates] + [to_far(e) for e in range(half)] + [to_x(d) for d in range(1, NX)]
     partners += [to_y(d) for d in range(1, NY)] + [to_core, to_zh]
     for partner in partners:
         pl.semaphore_signal(barrier, inc=1, device_id=partner, device_id_type=MESH)
@@ -280,8 +281,8 @@
 
     def own_step(i):
         e = order[i]
-        if e:
-            from_mate[e].wait_recv()
+        for copy in from_mate[e]:
+            copy.wait_recv()
         here = slot(core, x, e)
         for d in steps_x:
             along_x[i, d] = panels_to(here, 2, to_x(d))
@@ -311,10 +312,11 @@
         load_bias.wait()
         self_pre[0] = dot_nn(panels[own], ws_ref[...]) + bias_ref[...]
 
-    pair_copy = panels_to(own, 1, to_pair, dst=own + 1)
-    pair_copy.wait_recv()
     for e in mates:
-        from_mate[e] = panels_to(own, 2, to_mate(e), dst=slot(core, x, e))
+        from_mate[e] = [panels_to(own, 1, to_mate(e), dst=slot(core, x, e))]
+    from_mate[0] = [panels_to(own, 1, to_pair, dst=own + 1)]
+    for e in mates:
+        from_mate[e].append(panels_to(own, 1, to_far(e), dst=slot(core, x, e, 1)))
     for i in range(half + 2):
         if i < half:
             own_step(i)
@@ -447,7 +449,7 @@
         mine = col_sum(slot(core, turn_x(d), 0) + i, p)
         return mine + core_recv[p, turns.index(d) * nz + i].astype(F32)
 
-    core_copies, x_copies, quad_copies, pair_copies = {}, {}, {}, {}
+    core_copies, x_copies, z_copies = {}, {}, {}
 
     def core_stage(p):
         for at, d in enumerate(turns):
@@ -473,30 +475,22 @@
             value = value + x_recv[p, at, i].astype(F32)
         return value
 
-    def quad_stage(p):
+    def z_stage(p):
         for d in steps_x:
             x_copies[p, d].wait_recv()
-        for e in mates:
-            for q in range(2):
-                quad_send[p, e, q] = z_total(p, 2 * e + q).astype(BF16)
-            quad_copies[p, e] = links.send(
-                quad_send.at[p, e], quad_recv.at[p, e], to_mate(half - e)
-            )
-
-    def pair_stage(p):
-        value = z_total(p, 1)
-        for e in mates:
-            quad_copies[p, e].wait_recv()
-            value = value + quad_recv[p, e, 1].astype(F32)
-        pair_send[p] = value.astype(BF16)
-        pair_copies[p] = links.send(pair_send.at[p], pair_recv.at[p], to_pair)
+        for q in (1, 0):
+            for e in mates if q == 0 else (2, 1, 3, 0):
+                z_send[p, q, e] = z_total(p, 2 * e + q).astype(BF16)
+                to = to_far(half - e) if q else to_mate(half - e)
+                z_copies[p, q, e] = links.send(z_send.at[p, q, e], z_recv.at[p, q, e], to)
 
     def last_stage(p):
         value = z_total(p, 0) + self_grad[lines(p), :]
-        for e in mates:
-            value = value + quad_recv[p, e, 0].astype(F32)
-        pair_copies[p].wait_recv()
-        return value + pair_recv[p].astype(F32)
+        for (part_of, q, e), copy in z_copies.items():
+            if part_of == p:
+                copy.wait_recv()
+                value = value + z_recv[p, q, e].astype(F32)
+        return value
 
     for copy in wz_copies:
         copy.wait_recv()
@@ -522,7 +516,7 @@
     wx_copies = [links.send(wx_recv.at[x], wx_recv.at[x], to_x(d)) for d in (2, 1, 3)]
 
     x_stage(1)
-    quad_stage(0)
+    z_stage(0)
 
     for copy in wx_copies:
         copy.wait_recv()
@@ -532,7 +526,6 @@
     wc_send[...] = w_part
     wc_copy = links.send(wc_send, wc_recv, to_core)
 
-    pair_stage(0)
 
     wc_copy.wait_recv()
     w_part = w_part + wc_recv[...]
@@ -546,12 +539,11 @@
         links.send(w_out.at[y, rows_here], w_out.at[y, rows_here], to_mate(e)) for e in mates
     ]
 
-    quad_stage(1)
+    z_stage(1)
     for copy in gz_copies:
         copy.wait_recv()
     gy_copies = [links.send(w_out.at[y], w_out.at[y], to_y(d)) for d in (2, 1, 3)]
-    pair_stage(1)
-    links.finish(len(links.copies) - 8)
+    links.finish(len(links.copies) - 12)
     grad = jnp.concatenate([last_stage(p) for p in range(parts)], axis=0)
     ingrad_ref[...] = jnp.transpose(grad).astype(BF16)
     store(ingrad_ref, ingrad_hbm)
@@ -649,10 +641,8 @@
             halves(NX * nz),
             halves(NX - 1, nz),
             halves(NX - 1, nz),
-            halves(half, 2),
-            halves(half, 2),
-            halves(),
-            halves(),
+            halves(2, half),
+            halves(2, half),
             pltpu.VMEM((4, BLK + 16, BLK), BF16),
             pltpu.VMEM((4, BLK + 16, BLK), BF16),
             pltpu.VMEM((half, part, BLK), F32),

time: 104 us -> 105 us (level)
  the two profiles are of different devices: /device:TPU:24 before, /device:TPU:1 now
where the time goes in v8:
time: 105 us; the launch traced here: 104 us
  Pallas kernels  104 us (99%)
    pallas_call x1, Pallas kernels, body(): pl.pallas_call(functools.partial(kernel, nz, tiles), out_shape=results, i...  102 us

profile of v8, /device:TPU:1, one launch (start us, length us, event | category | flops | bytes accessed | tf_op | source)
XLA Modules:
  0.0 104.5 jit_solution(6419775175923388202)
XLA Ops:
  0.6 102.1 %shard_map.119 = (bf16[128,256]{1,0:T(8,128)(2,1)}, bf16[128,128]{1,0:T(8,128)(2,1)}, f32[128,256]{1,0:T(8,128)}, f32[128,256]{1,0:T(8,128)}, f32[1,256]{1,0:T(1,128)}) custom-call(bf16[128,128]{1,0:T(8,128)(2,1)} %x_hbm.1, bf16[128,256]{1,0:T(8,128)(2,1)} %ws_hbm.1, bf16[128,256]{1,0:T(8,128)(2,1)} %wn_hbm.1, f32[1,256]{1,0:T(1,128)} %bitcast.4, ...), custom_call_target="tpu_custom_call" | custom-call | flops 939524096 | bytes 3670016 | tf_op jit(solution)/shard_map/pallas_call | solution.py:615
  102.7 1.8 %shard_map.120 = (bf16[128,256]{1,0:T(8,128)(2,1)}, bf16[128,128]{1,0:T(8,128)(2,1)}, f32[128,256]{1,0:T(8,128)}, f32[128,256]{1,0:T(8,128)}, f32[1,256]{1,0:T(1,128)}) custom-call(bf16[128,256]{1,0:T(8,128)(2,1)} %get-tuple-element.15.refs_0_, bf16[128,128]{1,0:T(8,128)(2,1)} %get-tuple-element.16.refs_1_, f32[128,256]{1,0:T(8,128)} %get-tuple-element.17.refs_2_, ...), custom_call_target="tpu_custom_call" | custom-call | tf_op jit(solution)/shard_map/pallas_call | solution.py:679
